TPU v7x, 128 devices: a whole 4x4x4 slice. The times are simulated.
128 devices in a mesh: replica: 8 (over z, core), shard: 16 (over x, y).
Axes of the slice: x: 4, y: 4, z: 4, core: 2. Of those that a mesh axis runs over, the one named last changes fastest.
Arguments:
- grads: bfloat16 [8, 32, 1024, 1024], P('replica', 'shard')
- second_moment: float32 [32, 1024, 1024], P('shard', 'replica'), may hold values from 0.03 to 0.3
- left_stats: float32 [64, 1024, 1024], P('shard', 'replica')
- right_stats: float32 [64, 1024, 1024], P('shard', 'replica')
- left_root: bfloat16 [64, 1024, 1024], P('shard', 'replica'), as said below
- right_root: bfloat16 [64, 1024, 1024], P('shard', 'replica'), as said below
- owner_blocks: int32 [16, 4], replicated, may hold values from 0 to 32, as said below
Outputs:
- update: float32 [32, 1024, 1024], P('shard', 'replica')
- moment_new: float32 [32, 1024, 1024], P('shard', 'replica')
- left_new: float32 [64, 1024, 1024], P('shard', 'replica')
- right_new: float32 [64, 1024, 1024], P('shard', 'replica')
Inputs may be any that keep to these rules, and one draw needn't show every extreme that they name: Every block number below 32 appears exactly once in owner_blocks; the value 32 marks an empty entry, and an owner's blocks come before its empty entries. Block b lies on shard device b // 2, and no owner's list holds two blocks of the same shard device. `right_root`: each 1024 x 1024 block is symmetric. `left_root`: each 1024 x 1024 block is symmetric.
All inputs are finite; a program needn't handle non-finite values.
Results may differ from a plain program's by a relative error of at most 0.0041.
Values may be sent and summed in bfloat16 or wider, within the bound.
A program may use at most 128 MiB of HBM per device.

v0:
```python
import jax
import jax.numpy as jnp
from jax import lax
from jax.sharding import PartitionSpec as P

BETA_STAT = 0.99
BETA_MOMENT = 0.95
EPS_ADAM = 1e-08
EPS_NORM = 1e-06


def body(grads, second_moment, left_stats, right_stats, left_root, right_root, owner_blocks):
    shards = lax.axis_size("shard")
    myself = lax.axis_index("shard")
    replicas = lax.axis_size("replica")
    replica_id = lax.axis_index("replica")
    local_grads = grads[0]
    blocks_here = local_grads.shape[0]
    width = local_grads.shape[2]
    band = width // replicas
    entries = owner_blocks.shape[1]
    total_blocks = blocks_here * shards
    summed = lax.psum_scatter(
        local_grads.astype(jnp.float32), "replica", scatter_dimension=1, tiled=True
    )
    moment_new = BETA_MOMENT * second_moment + (1.0 - BETA_MOMENT) * summed * summed
    adam = summed / (jnp.sqrt(moment_new) + EPS_ADAM)
    adam_squares = jnp.sum(adam * adam, axis=(1, 2))
    grad_round = summed.astype(jnp.bfloat16)
    own_ids = myself * blocks_here + jnp.arange(blocks_here, dtype=jnp.int32)
    owned_here = jnp.any(owner_blocks[None, :, :] == own_ids[:, None, None], axis=2)
    owner_of = jnp.argmax(owned_here, axis=1)
    slot_ids = lax.dynamic_index_in_dim(owner_blocks, myself, 0, keepdims=False)
    live = slot_ids < total_blocks
    source = jnp.minimum(slot_ids, total_blocks - 1) // blocks_here
    initial = jnp.zeros((entries, band, width), jnp.bfloat16)
    piece = lax.all_gather(grad_round, "shard", axis=0, tiled=True)
    count = piece.shape[0]
    inside = live & (slot_ids >= 0) & (slot_ids < count)
    taken = piece[jnp.clip(slot_ids, 0, count - 1)]
    slot_rows = jnp.where(inside[:, None, None], taken, initial)
    slot_full = lax.all_gather(slot_rows, "replica", axis=1, tiled=True)
    left_new = BETA_STAT * left_stats + (1.0 - BETA_STAT) * jnp.einsum(
        "qrc,qkc->qrk", slot_rows, slot_full, preferred_element_type=jnp.float32
    )
    column_band = lax.dynamic_slice_in_dim(slot_full, replica_id * band, band, 2)
    right_new = BETA_STAT * right_stats + (1.0 - BETA_STAT) * jnp.einsum(
        "qkr,qkc->qrc", column_band, slot_full, preferred_element_type=jnp.float32
    )
    root_full = lax.all_gather(right_root, "replica", axis=1, tiled=True)
    product_full = jnp.einsum(
        "qkc,qcm->qkm", slot_full, root_full, preferred_element_type=jnp.float32
    ).astype(jnp.bfloat16)
    slot_precond = jnp.einsum(
        "qrk,qkm->qrm", left_root, product_full, preferred_element_type=jnp.float32
    )
    back_match = (source[None, :] == jnp.arange(shards, dtype=jnp.int32)[:, None]) & live[None, :]
    back_pick = jnp.argmax(back_match, axis=1)
    back_present = jnp.any(back_match, axis=1)
    returning = jnp.where(back_present[:, None, None], slot_precond[back_pick], 0.0)
    returned = lax.all_to_all(returning, "shard", split_axis=0, concat_axis=0, tiled=True)
    precond = returned[owner_of]
    pre_squares = jnp.sum(precond * precond, axis=(1, 2))
    adam_total, pre_total = lax.psum((adam_squares, pre_squares), "replica")
    scaling = jnp.sqrt(adam_total) / (jnp.sqrt(pre_total) + EPS_NORM)
    update = precond * scaling[:, None, None]
    return (update, moment_new, left_new, right_new)


def solution(mesh):
    in_specs = (
        P("replica", "shard", None, None),
        P("shard", "replica", None),
        P("shard", "replica", None),
        P("shard", "replica", None),
        P("shard", "replica", None),
        P("shard", "replica", None),
        P(),
    )
    out_specs = (
        P("shard", "replica", None),
        P("shard", "replica", None),
        P("shard", "replica", None),
        P("shard", "replica", None),
    )
    return jax.shard_map(body, mesh=mesh, in_specs=in_specs, out_specs=out_specs, check_vma=False)
```

profile of v0, /device:TPU:1, one launch (start us, length us, event | category | flops | bytes accessed | tf_op | source)
XLA Modules:
  0.0 451.4 jit_solution(5818570024412426336)
XLA Ops:
  7.2 0.0 reduce-scatter.2.cloned.1.call-start
  7.2 6.6 %bitcast_convert_fusion = f32[2,1024,1024]{2,1,0:T(8,128)} fusion(bf16[1,2,1024,1024]{3,2,1,0:T(8,128)(2,1)} %param.7), kind=kLoop, calls=%fused_computation.6 | loop fusion | flops 2097152 | bytes 12582912 | tf_op jit(solution)/shard_map/convert_element_type | solution.py:24
  13.8 0.0 reduce-scatter.2.cloned.1.call-update
  13.9 0.0 all-gather.4.cloned.1.call-start
  13.9 55.2 %reduce-scatter.2.cloned.1.call-done = f32[2,128,1024]{2,1,0:T(8,128)} async-done(((f32[2,1024,1024]{2,1,0:T(8,128)}), f32[2,128,1024]{2,1,0:T(8,128)}) %reduce-scatter.2.cloned.1.call-update) | async-done | bytes 1048592 | tf_op jit(solution)/shard_map/reduce_scatter | solution.py:23
  69.2 3.4 multiply_reduce_fusion.1
  72.6 0.0 all-gather.8.cloned.1.call-start
  72.6 0.7 all-gather.8.cloned.1.call-update
  73.3 0.0 all-gather.6.cloned.1.call-start
  73.4 0.2 compare_reduce_fusion.1
  73.6 0.2 fusion.10
  73.8 69.7 %all-gather.4.cloned.1.call-done = bf16[32,128,1024]{2,1,0:T(8,128)(2,1)} async-done(((bf16[2,128,1024]{2,1,0:T(8,128)(2,1)}), bf16[32,128,1024]{2,1,0:T(8,128)(2,1)}) %all-gather.4.cloned.1.call-update) | async-done | bytes 8388624 | tf_op jit(solution)/shard_map/all_gather | solution.py:37
  143.5 4.0 gather_fusion
  147.5 1.1 broadcast_select_fusion.1
  148.7 0.6 iota_reduce_fusion
  149.3 0.1 fusion.13
  149.4 46.0 %all-gather.8.cloned.1.call-done = bf16[4,1024,1024]{2,1,0:T(8,128)(2,1)} async-done(((bf16[4,128,1024]{2,1,0:T(8,128)(2,1)}), bf16[4,1024,1024]{2,1,0:T(8,128)(2,1)}) %all-gather.8.cloned.1.call-update) | async-done | bytes 8388624 | tf_op jit(solution)/shard_map/all_gather | solution.py:50
  195.3 52.1 %all-gather.6.cloned.1.call-done = bf16[4,1024,1024]{2,1,0:T(8,128)(2,1)} async-done(((bf16[4,128,1024]{2,1,0:T(8,128)(2,1)}), bf16[4,1024,1024]{2,1,0:T(8,128)(2,1)}) %all-gather.6.cloned.1.call-update) | async-done | bytes 8388624 | tf_op jit(solution)/shard_map/all_gather | solution.py:42
  247.5 14.7 %fusion.4 = f32[4,128,1024]{1,2,0:T(8,128)S(1)} fusion(bf16[4,128,1024]{2,1,0:T(8,128)(2,1)S(1)} %copy-done, bf16[4,1024,1024]{2,1,0:T(8,128)(2,1)} %all-gather.6.cloned.1.call-done, bf16[4,1024,1024]{2,1,0:T(8,128)(2,1)} %all-gather.8.cloned.1.call-done), kind=kOutput, calls=%fused_computation.10 | convolution fusion | flops 9667870720 | bytes 19922944 | tf_op jit(solution)/shard_map/qrk,qkm->qrm/dot_general | solution.py:54
  262.1 4.3 gather_fusion.1
  266.4 7.5 %broadcast_select_fusion = f32[16,128,1024]{1,2,0:T(8,128)} fusion(f32[16,128,1024]{1,2,0:T(8,128)} %gather_fusion.1, pred[16]{0:T(512)(128)(4,1)S(1)} %fusion.13), kind=kLoop, calls=%fused_computation.7 | loop fusion | flops 2097152 | bytes 16777232 | tf_op jit(solution)/shard_map/jit(_where)/select_n | solution.py:60
  273.9 6.6 %all-to-all-start = ((f32[16,128,1024]{1,2,0:T(8,128)}), f32[16,128,1024]{1,2,0:T(8,128)}, u32[]{:S(2)}, u32[]{:S(2)}) async-start(f32[16,128,1024]{1,2,0:T(8,128)} %broadcast_select_fusion), calls=%async_computation.1 | async-start | bytes 16777216 | tf_op jit(solution)/shard_map/all_to_all | solution.py:61
  280.5 0.1 compare_reduce_fusion
  280.6 0.6 iota_reduce_fusion.1
  281.3 7.4 %multiply_add_fusion = f32[4,128,1024]{2,1,0:T(8,128)} fusion(f32[4,128,1024]{2,1,0:T(8,128)} %param.10, bf16[4,1024,1024]{2,1,0:T(8,128)(2,1)} %all-gather.6.cloned.1.call-done, s32[]{:T(128)S(6)} %select_n.52), kind=kOutput, calls=%fused_computation.8 | convolution fusion | flops 1075314688 | bytes 13631492 | tf_op jit(solution)/shard_map/qkr,qkc->qrc/dot_general | solution.py:47
  288.7 8.3 %multiply_add_fusion.1 = f32[4,128,1024]{2,1,0:T(8,128)} fusion(f32[4,128,1024]{2,1,0:T(8,128)} %param.9, bf16[4,128,1024]{2,1,0:T(8,128)(2,1)S(1)} %copy-done.2, bf16[4,1024,1024]{2,1,0:T(8,128)(2,1)} %all-gather.6.cloned.1.call-done), kind=kOutput, calls=%fused_computation.9 | convolution fusion | flops 1075314688 | bytes 13631488 | tf_op jit(solution)/shard_map/qrc,qkc->qrk/dot_general | solution.py:43
  296.9 129.4 %all-to-all-done = f32[16,128,1024]{1,2,0:T(8,128)} async-done(((f32[16,128,1024]{1,2,0:T(8,128)}), f32[16,128,1024]{1,2,0:T(8,128)}, u32[]{:S(2)}, u32[]{:S(2)}) %all-to-all-start) | async-done | bytes 8388640 | tf_op jit(solution)/shard_map/all_to_all | solution.py:61
  426.4 4.0 gather_fusion.2
  430.4 0.2 multiply_reduce_fusion
  430.6 12.8 %all-reduce = (f32[2]{0:T(128)S(1)}, f32[2]{0:T(128)S(1)}) all-reduce(f32[2]{0:T(128)S(1)} %multiply_reduce_fusion, f32[2]{0:T(128)S(1)} %get-tuple-element.26), channel_id=1, replica_groups=mesh['replica'=8,'shard'=16] {'replica'}, use_global_device_ids=true, to_apply=%region_8.9 | all-reduce | flops 4 | bytes 32 | tf_op jit(solution)/shard_map/psum | solution.py:64
  443.4 0.1 broadcast_multiply_fusion
  443.6 1.3 copy.19
  (21 shorter events, 0.1 us)
Async XLA Ops:
  7.2 240.3 %copy-start = (bf16[4,128,1024]{2,1,0:T(8,128)(2,1)S(1)}, bf16[4,128,1024]{2,1,0:T(8,128)(2,1)}, u32[]{:S(2)}) copy-start(bf16[4,128,1024]{2,1,0:T(8,128)(2,1)} %param.11) | copy-start | bytes 3145732
  7.2 62.0 %copy-start.3 = (f32[2,128,1024]{2,1,0:T(8,128)S(1)}, f32[2,128,1024]{2,1,0:T(8,128)}, u32[]{:S(2)}) copy-start(f32[2,128,1024]{2,1,0:T(8,128)} %param.8) | copy-start | bytes 3145732
  7.2 62.0 %reduce-scatter.2.cloned.1.call-start = ((), (), s32[]{:S(2)}) async-start(), calls=%async_computation.2 | async-start | bytes 9437184 | tf_op jit(solution)/shard_map/reduce_scatter | solution.py:23
  13.8 59.5 %copy-start.4 = (s32[16,4]{0,1:T(4,128)S(1)}, s32[16,4]{0,1:T(4,128)}, u32[]{:S(2)}) copy-start(s32[16,4]{0,1:T(4,128)} %param.13) | copy-start | bytes 772
  13.9 129.7 %all-gather.4.cloned.1.call-start = ((), (), s32[]{:S(2)}) async-start(), calls=%async_computation.3 | async-start | bytes 8912896 | tf_op jit(solution)/shard_map/all_gather | solution.py:37
  72.6 122.8 %all-gather.8.cloned.1.call-start = ((), (), s32[]{:S(2)}) async-start(), calls=%async_computation.5 | async-start | bytes 9437184 | tf_op jit(solution)/shard_map/all_gather | solution.py:50
  73.3 174.1 %all-gather.6.cloned.1.call-start = ((), (), s32[]{:S(2)}) async-start(), calls=%async_computation.4 | async-start | bytes 9437184 | tf_op jit(solution)/shard_map/all_gather | solution.py:42
  273.9 152.5 %all-to-all-start = ((f32[16,128,1024]{1,2,0:T(8,128)}), f32[16,128,1024]{1,2,0:T(8,128)}, u32[]{:S(2)}, u32[]{:S(2)}) async-start(f32[16,128,1024]{1,2,0:T(8,128)} %broadcast_select_fusion), calls=%async_computation.1 | async-start | bytes 16777216 | tf_op jit(solution)/shard_map/all_to_all | solution.py:61
  280.5 8.1 %copy-start.2 = (bf16[4,128,1024]{2,1,0:T(8,128)(2,1)S(1)}, bf16[4,128,1024]{2,1,0:T(8,128)(2,1)}, u32[]{:S(2)}) copy-start(bf16[4,128,1024]{2,1,0:T(8,128)(2,1)} %broadcast_select_fusion.1) | copy-start | bytes 3145732
  281.3 163.6 %copy-start.1 = (bf16[4,128,1024]{2,1,0:T(8,128)(2,1)S(1)}, bf16[4,128,1024]{2,1,0:T(8,128)(2,1)}, u32[]{:S(2)}) copy-start(bf16[4,128,1024]{2,1,0:T(8,128)(2,1)} %param.11) | copy-start | bytes 3145732
Sparse Core Ops, SparseCore 0:
  14.0 55.1 reduce-scatter.1
  72.7 70.7 all-gather.3
  145.2 50.0 all-gather.7
  197.5 49.9 all-gather.5
where the time goes:
time: 456 us; the launch traced here: 451 us
  waiting for transfers between devices  353 us (77%)
  matrix products  30.3 us (7%)
  other arithmetic  20.8 us (5%)
  between operations  13.9 us (3%)
  local copies, waits for them, and re-layouts  13.6 us (3%)
  blocking collectives  12.8 us (3%)
  starting transfers between devices  6.75 us (1%)
    all_to_all x1, waiting for transfers between devices, body(): lax.all_to_all(returning, 'shard', split_axis=0, concat_axis=0, tiled=True)  129 us
    all_gather x1, waiting for transfers between devices, body(): piece = lax.all_gather(grad_round, 'shard', axis=0, tiled=True)  69.7 us
    reduce_scatter x1, waiting for transfers between devices, body(): lax.psum_scatter(local_grads.astype(jnp.float32), 'replica', scatter_dime...  55.2 us
    all_gather x1, waiting for transfers between devices, body(): slot_full = lax.all_gather(slot_rows, 'replica', axis=1, tiled=True)  52.1 us
    all_gather x1, waiting for transfers between devices, body(): root_full = lax.all_gather(right_root, 'replica', axis=1, tiled=True)  46 us
    dot_general x1, matrix products, body(): jnp.einsum('qrk,qkm->qrm', left_root, product_full, preferred_element_typ...  14.7 us
    psum x1, blocking collectives, body(): adam_total, pre_total = lax.psum((adam_squares, pre_squares), 'replica')  12.8 us
  transfers between devices with their start and end apart: 5, of which 5 were waited for; matrix products, arithmetic and copies ran while one was open for 5% of the time, Pallas kernels for 0%

commit v1 on v0

v1 whole, which is shorter than its diff:
```python
import functools

import jax
import jax.numpy as jnp
from jax import lax
from jax.experimental import pallas as pl
from jax.experimental.pallas import tpu as pltpu
from jax.sharding import PartitionSpec as P

BETA_STAT = 0.99
BETA_MOMENT = 0.95
EPS_ADAM = 1e-08
EPS_NORM = 1e-06
MESH = pl.DeviceIdType.MESH

NS = 4
NK = 2
Q = 4


def flip(v, low, high):
    if low:
        v = v + 1 - 2 * (v % 2)
    if high:
        v = 3 - v
    return v


def gray_bits(v):
    return ((v + 1) // 2) % 2, v // 2


def kernel(
    ob_ref, inv_ref, grads, sm_hbm, lroot, rroot,
    update_out, moment_out, gl_out, gr_out,
    far0, far1, sm0, sm1, nr0, nr1, so, mg0, mg1, ms0, ms1, own0, own1, ownb,
    smv, mom, gf, rf, tb, pv, lh, nsend, nrecv,
    r_own, r_v0, r_sa, r_ra, r_sb, r_rb, r_sc, r_rc,
    l_own, l_v0, l_sa, l_ra, l_sb, l_rb, l_sc, l_rc,
    gl_h, gl_s, gl_r, gl_o, gr_h, gr_s, gr_r, gr_o,
    loc_sem, a_ss, a_rs, gag_ss, gag_rs, rag_ss, rag_rs,
    rp_ss, rp_rs, lp_ss, lp_rs, glp_ss, glp_rs, grp_ss, grp_rs, n_ss, n_rs,
):
    band = sm_hbm.shape[1]
    width = sm_hbm.shape[2]
    part = band // Q
    r = lax.axis_index("replica")
    s = lax.axis_index("shard")
    z, c = r // 2, r % 2
    x, y = s // 4, s % 4
    zp, zm, zf = (z + 1) % 4, (z + 3) % 4, (z + 2) % 4
    sib = 1 - c

    def dev(zz, cc):
        return (zz * 2 + cc, s)

    def rows(zz, cc):
        return pl.ds((zz * 2 + cc) * band, band)

    def shard_at(flips):
        return 4 * flip(x, 2 in flips, 3 in flips) + flip(y, 0 in flips, 1 in flips)

    def across(dim):
        return (r, shard_at((dim,)))

    def bits(shard):
        ya, yb = gray_bits(shard % 4)
        xa, xb = gray_bits(shard // 4)
        return (ya, yb, xa, xb)

    mine = bits(s)

    def remote(src, dst, ss, rs, to):
        return pltpu.make_async_remote_copy(
            src_ref=src, dst_ref=dst, send_sem=ss, recv_sem=rs, device_id=to, device_id_type=MESH
        )

    me = (r, s)

    def arrived(dst, ss, rs, to):
        remote(dst, dst, ss, rs, to).wait_recv()

    sends = []

    def go(cp):
        cp.start()
        sends.append(cp)

    locs = [
        pltpu.make_async_copy(grads.at[0, 0, rows(zm, c)], own0, loc_sem.at[0]),
        pltpu.make_async_copy(grads.at[0, 1, rows(zp, c)], own1, loc_sem.at[1]),
        pltpu.make_async_copy(grads.at[0, :, rows(z, c)], ownb, loc_sem.at[2]),
        pltpu.make_async_copy(sm_hbm, smv, loc_sem.at[3]),
        pltpu.make_async_copy(rroot, r_own, loc_sem.at[4]),
        pltpu.make_async_copy(lroot, l_own, loc_sem.at[5]),
    ]
    for cp in locs:
        cp.start()

    barrier = pltpu.get_barrier_semaphore()
    partners = [dev(z, sib)] + [dev(zz, cc) for zz in (zm, zp, zf) for cc in (0, 1)]
    partners += [across(d) for d in range(4)]
    for p in partners:
        pl.semaphore_signal(barrier, inc=1, device_id=p, device_id_type=MESH)
    pl.semaphore_wait(barrier, len(partners))

    for j in (0, 1):
        go(remote(grads.at[0, 0, rows(zf, j)], far0.at[c], a_ss.at[0, j], a_rs.at[0, c], dev(zm, j)))
        go(remote(grads.at[0, 1, rows(zf, j)], far1.at[c], a_ss.at[1, j], a_rs.at[1, c], dev(zp, j)))
    go(remote(grads.at[0, 0, rows(zm, sib)], sm0, a_ss.at[2, 0], a_rs.at[2, 0], dev(z, sib)))
    go(remote(grads.at[0, 1, rows(zp, sib)], sm1, a_ss.at[2, 1], a_rs.at[2, 1], dev(z, sib)))
    go(remote(grads.at[0, :, rows(z, sib)], so, a_ss.at[3, 0], a_rs.at[3, 0], dev(z, sib)))

    class Inward:
        def __init__(self, root, own, v0, sa, ra, sb, rb, sc, rc, ss, rs):
            self.root, self.own, self.v0 = root, own, v0
            self.bufs = [(sa, ra), (sb, rb), (sc, rc)]
            self.ss, self.rs = ss, rs

        def order(self, j):
            return [(j + i) % 4 for i in range(4)]

        def start(self):
            for j in range(Q):
                d = self.order(j)
                go(remote(self.root.at[:, pl.ds(part * j, part)], self.v0.at[j],
                          self.ss.at[0, j], self.rs.at[0, j], across(d[3])))

        def wait(self, stage):
            for j in range(Q):
                d = self.order(j)
                dst = self.v0.at[j] if stage == 0 else self.bufs[stage - 1][1].at[j]
                arrived(dst, self.ss.at[stage, j], self.rs.at[stage, j], across(d[3 - stage]))

        def pick(self, j, level, home_flips, k, ea, eb):
            d = self.order(j)
            place = inv_ref[2 * shard_at(home_flips) + k]
            owner, slot = place // NS, place % NS
            theirs = bits(owner)
            value = jnp.where(theirs[d[3]] != mine[d[3]], self.v0[j, slot],
                              self.own[slot, pl.ds(part * j, part)])
            if level >= 1:
                value = jnp.where(theirs[d[2]] != mine[d[2]], self.bufs[0][1][j, ea], value)
            if level >= 2:
                value = jnp.where(theirs[d[1]] != mine[d[1]], self.bufs[1][1][j, eb], value)
            if level >= 3:
                value = jnp.where(theirs[d[0]] != mine[d[0]], self.bufs[2][1][j, k], value)
            return value

        def send(self, stage):
            src, dst = self.bufs[stage - 1]
            for j in range(Q):
                d = self.order(j)
                for e in range(8 >> (stage - 1)):
                    k, r0, r1 = e % 2, (e // 2) % 2, e // 4
                    if stage == 1:
                        flips = (d[2],) + ((d[0],) if r0 else ()) + ((d[1],) if r1 else ())
                        ea = eb = None
                    elif stage == 2:
                        flips = (d[1],) + ((d[0],) if r0 else ())
                        ea, eb = 4 + 2 * r0 + k, None
                    else:
                        flips = (d[0],)
                        ea, eb = 2 + k, 2 + k
                    src[j, e] = self.pick(j, stage - 1, flips, k, ea, eb)
                go(remote(src.at[j], dst.at[j], self.ss.at[stage, j], self.rs.at[stage, j], across(d[3 - stage])))

        def finish(self, put):
            for j in range(Q):
                for k in range(NK):
                    put(j, k, self.pick(j, 3, (), k, k, k))

    right = Inward(rroot, r_own, r_v0, r_sa, r_ra, r_sb, r_rb, r_sc, r_rc, rp_ss, rp_rs)
    left = Inward(lroot, l_own, l_v0, l_sa, l_ra, l_sb, l_rb, l_sc, l_rc, lp_ss, lp_rs)
    right.start()
    left.start()

    for j in (0, 1):
        go(remote(grads.at[0, 1, rows(zm, j)], nr1.at[c], a_ss.at[4, j], a_rs.at[4, c], dev(zm, j)))
        go(remote(grads.at[0, 0, rows(zp, j)], nr0.at[c], a_ss.at[5, j], a_rs.at[5, c], dev(zp, j)))

    locs[4].wait()
    right.wait(0)
    right.send(1)

    for cc in (0, 1):
        arrived(far0.at[cc], a_ss.at[0, cc], a_rs.at[0, cc], dev(zm, cc))
        arrived(far1.at[cc], a_ss.at[1, cc], a_rs.at[1, cc], dev(zp, cc))
    arrived(sm0, a_ss.at[2, 0], a_rs.at[2, 0], dev(z, sib))
    arrived(sm1, a_ss.at[2, 1], a_rs.at[2, 1], dev(z, sib))
    locs[0].wait()
    locs[1].wait()
    step_rows = 16

    def f32(v):
        return v.astype(jnp.float32)

    @pl.loop(0, band // step_rows)
    def _(i):
        at = pl.ds(pl.multiple_of(i * step_rows, step_rows), step_rows)
        ms0[at] = (f32(own0[at]) + f32(sm0[at])) + (f32(far0[0, at]) + f32(far0[1, at]))
        ms1[at] = (f32(own1[at]) + f32(sm1[at])) + (f32(far1[0, at]) + f32(far1[1, at]))

    go(remote(ms0, mg0, a_ss.at[6, 0], a_rs.at[6, 0], dev(zm, c)))
    go(remote(ms1, mg1, a_ss.at[6, 1], a_rs.at[6, 1], dev(zp, c)))

    locs[5].wait()
    left.wait(0)
    left.send(1)
    right.wait(1)
    right.send(2)

    for cc in (0, 1):
        arrived(nr1.at[cc], a_ss.at[4, cc], a_rs.at[4, cc], dev(zm, cc))
        arrived(nr0.at[cc], a_ss.at[5, cc], a_rs.at[5, cc], dev(zp, cc))
    arrived(so, a_ss.at[3, 0], a_rs.at[3, 0], dev(z, sib))
    locs[2].wait()
    locs[3].wait()
    arrived(mg0, a_ss.at[6, 0], a_rs.at[6, 0], dev(zm, c))
    arrived(mg1, a_ss.at[6, 1], a_rs.at[6, 1], dev(zp, c))

    def fold(v):
        v = v[:8] + v[8:]
        total = v[:, :128]
        for i in range(1, width // 128):
            total = total + v[:, 128 * i:128 * (i + 1)]
        return total

    for k, near, merged in ((0, nr0, mg0), (1, nr1, mg1)):
        def one(i, acc, k=k, near=near, merged=merged):
            start = pl.multiple_of(i * step_rows, step_rows)
            at = pl.ds(start, step_rows)
            g = (f32(ownb[k, at]) + f32(so[k, at])) + (f32(near[0, at]) + f32(near[1, at])) + merged[at]
            m = BETA_MOMENT * smv[k, at] + (1.0 - BETA_MOMENT) * g * g
            mom[k, at] = m
            a = g / (jnp.sqrt(m) + EPS_ADAM)
            gf[k, pl.ds(pl.multiple_of(r * band + start, step_rows), step_rows)] = g.astype(jnp.bfloat16)
            return acc + fold(a * a)

        nsend[k] = lax.fori_loop(0, band // step_rows, one, jnp.zeros((8, 128), jnp.float32))

    class Gather:
        def __init__(self, buf, ss, rs):
            self.buf, self.ss, self.rs = buf, ss, rs

        def copy(self, i, k, zz, cc, to):
            piece = self.buf.at[k, rows(zz, cc)]
            return remote(piece, piece, self.ss.at[i], self.rs.at[i], to)

        def got(self, i, k, zz, cc, to):
            self.copy(i, k, zz, cc, to).wait_recv()

        def start(self):
            go(self.copy(0, 0, z, c, dev(zm, c)))
            go(self.copy(1, 1, z, c, dev(zp, c)))
            go(self.copy(2, 1, z, c, dev(zm, c)))
            go(self.copy(3, 0, z, c, dev(zp, c)))
            go(self.copy(4, 0, z, c, dev(z, sib)))
            go(self.copy(5, 1, z, c, dev(z, sib)))

        def forward(self):
            self.got(0, 0, zp, c, dev(zm, c))
            go(self.copy(6, 0, zp, c, dev(zm, c)))
            self.got(1, 1, zm, c, dev(zp, c))
            go(self.copy(7, 1, zm, c, dev(zp, c)))
            go(self.copy(8, 0, zp, c, dev(z, sib)))
            go(self.copy(9, 1, zm, c, dev(z, sib)))

        def rest(self):
            self.got(2, 1, zp, c, dev(zm, c))
            go(self.copy(10, 1, zp, c, dev(z, sib)))
            self.got(3, 0, zm, c, dev(zp, c))
            go(self.copy(11, 0, zm, c, dev(z, sib)))

        def last(self):
            self.got(6, 0, zf, c, dev(zm, c))
            go(self.copy(12, 0, zf, c, dev(z, sib)))
            self.got(7, 1, zf, c, dev(zp, c))
            go(self.copy(13, 1, zf, c, dev(z, sib)))

        def complete(self):
            for i, k, zz in ((4, 0, z), (5, 1, z), (8, 0, zp), (9, 1, zm), (10, 1, zp), (11, 0, zm), (12, 0, zf), (13, 1, zf)):
                self.got(i, k, zz, sib, dev(z, sib))

    gather_g = Gather(gf, gag_ss, gag_rs)
    gather_r = Gather(rf, rag_ss, rag_rs)
    gather_g.start()
    mom_cp = pltpu.make_async_copy(mom, moment_out, loc_sem.at[6])
    mom_cp.start()

    left.wait(1)
    left.send(2)
    right.wait(2)
    right.send(3)
    gather_g.forward()
    left.wait(2)
    left.send(3)
    gather_g.rest()
    right.wait(3)

    def put_right(j, k, value):
        rf[k, pl.ds(pl.multiple_of(r * band + part * j, part), part)] = value

    right.finish(put_right)
    gather_g.last()
    gather_r.start()
    gather_g.complete()

    class Outward:
        def __init__(self, held, src, dst, out, ss, rs):
            self.held, self.src, self.dst, self.out, self.ss, self.rs = held, src, dst, out, ss, rs

        def order(self, j):
            return [(j + i) % 4 for i in range(4)]

        def spread(self, stage):
            n = 2 << stage
            for j in range(Q):
                d = self.order(j)
                go(remote(self.held.at[j, pl.ds(0, n)], self.held.at[j, pl.ds(n, n)],
                          self.ss.at[stage, j], self.rs.at[stage, j], across(d[stage])))

        def wait(self, stage):
            n = 2 << stage
            for j in range(Q):
                d = self.order(j)
                dst = self.dst.at[j] if stage == 3 else self.held.at[j, pl.ds(n, n)]
                arrived(dst, self.ss.at[stage, j], self.rs.at[stage, j], across(d[stage]))

        def look(self, j, owner, q):
            d = self.order(j)
            block = ob_ref[owner * NS + q]
            safe = jnp.minimum(block, 31)
            theirs = bits(safe // 2)
            differ = [jnp.where(theirs[t] != mine[t], 1, 0) for t in d]
            entry = 2 * (differ[0] + 2 * differ[1] + 4 * differ[2]) + safe % 2
            return block, differ[3], self.held[j, entry]

        def send(self):
            for j in range(Q):
                d = self.order(j)
                for q in range(NS):
                    self.src[j, q] = self.look(j, shard_at((d[3],)), q)[2]
                go(remote(self.src.at[j], self.dst.at[j], self.ss.at[3, j], self.rs.at[3, j], across(d[3])))

        def finish(self):
            for j in range(Q):
                for q in range(NS):
                    block, far, here = self.look(j, s, q)
                    value = jnp.where(far == 1, self.dst[j, q], here)
                    value = jnp.where(block < 32, value, jnp.zeros_like(value))
                    self.out[q, pl.ds(part * j, part)] = value

    out_l = Outward(gl_h, gl_s, gl_r, gl_o, glp_ss, glp_rs)
    out_r = Outward(gr_h, gr_s, gr_r, gr_o, grp_ss, grp_rs)

    tile = 256
    mm = functools.partial(lax.dot_general, preferred_element_type=jnp.float32)
    for k in range(NK):
        band_rows = gf[k, pl.ds(pl.multiple_of(r * band, band), band)]

        @pl.loop(0, width // tile)
        def _(i, k=k, band_rows=band_rows):
            at = pl.ds(pl.multiple_of(i * tile, tile), tile)
            g = mm(band_rows, gf[k, at], (((1,), (1,)), ((), ()))).astype(jnp.bfloat16)
            for j in range(Q):
                gl_h[j, k, :, at] = g[part * j:part * (j + 1)]

    out_l.spread(0)
    for k in range(NK):
        cols = gf[k, :, pl.ds(pl.multiple_of(r * band, band), band)].T

        @pl.loop(0, width // tile)
        def _(i, k=k, cols=cols):
            at = pl.ds(pl.multiple_of(i * tile, tile), tile)
            g = mm(cols, gf[k, :, at], (((1,), (0,)), ((), ()))).astype(jnp.bfloat16)
            for j in range(Q):
                gr_h[j, k, :, at] = g[part * j:part * (j + 1)]

    out_r.spread(0)

    left.wait(3)

    def put_left(j, k, value):
        lh[k, pl.ds(part * j, part)] = value

    left.finish(put_left)

    out_l.wait(0)
    out_l.spread(1)
    out_r.wait(0)
    out_r.spread(1)
    gather_r.forward()
    out_l.wait(1)
    out_l.spread(2)
    gather_r.rest()
    gather_r.last()
    out_r.wait(1)
    out_r.spread(2)
    gather_r.complete()

    for k in range(NK):
        @pl.loop(0, width // tile)
        def _(i, k=k):
            at = pl.ds(pl.multiple_of(i * tile, tile), tile)
            tb[at] = mm(gf[k, at], rf[k], (((1,), (0,)), ((), ()))).astype(jnp.bfloat16)

        @pl.loop(0, width // tile)
        def _(i, k=k):
            at = pl.ds(pl.multiple_of(i * tile, tile), tile)
            pv[k, :, at] = mm(lh[k], tb[:, at], (((1,), (0,)), ((), ())))

        def square(i, acc, k=k):
            v = pv[k, pl.ds(pl.multiple_of(i * step_rows, step_rows), step_rows)]
            return acc + fold(v * v)

        nsend[NK + k] = lax.fori_loop(0, band // step_rows, square, jnp.zeros((8, 128), jnp.float32))

    others = [(z, sib, 0)] + [(zz, cc, 1 + 2 * i + cc) for i, zz in enumerate((zm, zp, zf)) for cc in (0, 1)]
    for zz, cc, i in others:
        go(remote(nsend, nrecv.at[r], n_ss.at[i], n_rs.at[r], dev(zz, cc)))
    for zz, cc, i in others:
        src = zz * 2 + cc
        arrived(nrecv.at[src], n_ss.at[i], n_rs.at[src], dev(zz, cc))
    nrecv[r] = nsend[...]
    sums = nrecv[0]
    for i in range(1, 8):
        sums = sums + nrecv[i]
    for k in range(NK):
        adam_total = jnp.sum(sums[k], keepdims=True)
        pre_total = jnp.sum(sums[NK + k], keepdims=True)
        scaling = jnp.sqrt(adam_total) / (jnp.sqrt(pre_total) + EPS_NORM)

        @pl.loop(0, band // step_rows)
        def _(i, k=k, scaling=scaling):
            at = pl.ds(pl.multiple_of(i * step_rows, step_rows), step_rows)
            pv[k, at] = pv[k, at] * scaling

    up_cp = pltpu.make_async_copy(pv, update_out, loc_sem.at[7])
    up_cp.start()

    out_l.wait(2)
    out_l.send()
    out_r.wait(2)
    out_r.send()
    out_l.wait(3)
    out_l.finish()
    gl_cp = pltpu.make_async_copy(gl_o, gl_out, loc_sem.at[8])
    gl_cp.start()
    out_r.wait(3)
    out_r.finish()
    gr_cp = pltpu.make_async_copy(gr_o, gr_out, loc_sem.at[9])
    gr_cp.start()

    for cp in sends:
        cp.wait_send()
    for cp in (mom_cp, up_cp, gl_cp, gr_cp):
        cp.wait()


def body(grads, second_moment, left_stats, right_stats, left_root, right_root, owner_blocks):
    bf16, f32 = jnp.bfloat16, jnp.float32
    band, width = second_moment.shape[1], second_moment.shape[2]
    full = 8 * band
    part = band // Q
    table = owner_blocks.reshape(-1)
    blocks = jnp.arange(32, dtype=jnp.int32)
    inverse = jnp.sum(
        jnp.where(table[None, :] == blocks[:, None], jnp.arange(64, dtype=jnp.int32)[None, :], 0), axis=1
    )
    V, D = pltpu.VMEM, pltpu.SemaphoreType.DMA
    inward = [
        V((NS, band, width), bf16), V((Q, NS, part, width), bf16),
        V((Q, 8, part, width), bf16), V((Q, 8, part, width), bf16),
        V((Q, 4, part, width), bf16), V((Q, 4, part, width), bf16),
        V((Q, 2, part, width), bf16), V((Q, 2, part, width), bf16),
    ]
    outward = [
        V((Q, 16, part, width), bf16), V((Q, NS, part, width), bf16),
        V((Q, NS, part, width), bf16), V((NS, band, width), bf16),
    ]
    scratch = (
        [V((2, band, width), bf16)] * 2
        + [V((band, width), bf16)] * 2
        + [V((2, band, width), bf16)] * 2
        + [V((2, band, width), bf16)]
        + [V((band, width), f32)] * 4
        + [V((band, width), bf16)] * 2
        + [V((2, band, width), bf16)]
        + [V((2, band, width), f32)] * 2
        + [V((2, full, width), bf16)] * 2
        + [V((full, width), bf16)]
        + [V((2, band, width), f32)]
        + [V((2, band, width), bf16)]
        + [V((4, 8, 128), f32), V((8, 4, 8, 128), f32)]
        + inward + inward + outward + outward
        + [D((10,)), D((7, 2)), D((7, 2)), D((14,)), D((14,)), D((14,)), D((14,))]
        + [D((4, Q))] * 8
        + [D((7,)), D((8,))]
    )
    hbm = pl.BlockSpec(memory_space=pl.ANY)
    smem = pl.BlockSpec(memory_space=pltpu.SMEM)
    update, moment_new, gram_left, gram_right = pl.pallas_call(
        kernel,
        out_shape=(
            jax.ShapeDtypeStruct((2, band, width), f32),
            jax.ShapeDtypeStruct((2, band, width), f32),
            jax.ShapeDtypeStruct((NS, band, width), bf16),
            jax.ShapeDtypeStruct((NS, band, width), bf16),
        ),
        in_specs=[smem, smem, hbm, hbm, hbm, hbm],
        out_specs=(hbm, hbm, hbm, hbm),
        scratch_shapes=scratch,
        compiler_params=pltpu.CompilerParams(
            collective_id=0, has_side_effects=True, vmem_limit_bytes=60 * 2**20
        ),
        name="shampoo",
    )(table, inverse, grads, second_moment, left_root, right_root)
    left_new = BETA_STAT * left_stats + (1.0 - BETA_STAT) * gram_left.astype(f32)
    right_new = BETA_STAT * right_stats + (1.0 - BETA_STAT) * gram_right.astype(f32)
    return (update, moment_new, left_new, right_new)


def solution(mesh):
    in_specs = (
        P("replica", "shard", None, None),
        P("shard", "replica", None),
        P("shard", "replica", None),
        P("shard", "replica", None),
        P("shard", "replica", None),
        P("shard", "replica", None),
        P(),
    )
    out_specs = (
        P("shard", "replica", None),
        P("shard", "replica", None),
        P("shard", "replica", None),
        P("shard", "replica", None),
    )
    return jax.shard_map(body, mesh=mesh, in_specs=in_specs, out_specs=out_specs, check_vma=False)
```

time: 456 us -> 135 us (0.30)
  waiting for transfers between devices: 353 us -> 0 us
  Pallas kernels: 0 us -> 124 us
  matrix products: 30.3 us -> 0 us
  other arithmetic: 20.8 us -> 6.03 us
  between operations: 13.9 us -> 0.67 us
  blocking collectives: 12.8 us -> 0 us
  local copies, waits for them, and re-layouts: 13.6 us -> 3.43 us
  starting transfers between devices: 6.75 us -> 0 us
    all_gather x3 -> x0, waiting for transfers between devices: 168 us -> none  [the longest x1 69.7 us: body(): piece = lax.all_gather(grad_round, 'shard', axis=0, tiled=True)]
    all_to_all x1 -> x0, waiting for transfers between devices: 129 us -> none  [body(): lax.all_to_all(returning, 'shard', split_axis=0, concat_axis=0, tiled=True)]
    pallas_call x0 -> x1, Pallas kernels: none -> 124 us  [body(): pl.pallas_call(kernel, out_shape=(jax.ShapeDtypeStruct((2, band, width),...]
    reduce_scatter x1 -> x0, waiting for transfers between devices: 55.2 us -> none  [body(): lax.psum_scatter(local_grads.astype(jnp.float32), 'replica', scatter_dime...]
    dot_general x3 -> x0, matrix products: 30.3 us -> none  [the longest x1 14.7 us: body(): jnp.einsum('qrk,qkm->qrm', left_root, product_full, preferred_element_typ...]
    psum x1 -> x0, blocking collectives: 12.8 us -> none  [body(): adam_total, pre_total = lax.psum((adam_squares, pre_squares), 'replica')]
    gather x3 -> x0, local copies, waits for them, and re-layouts: 12.3 us -> none  [the longest x1 4.31 us: body(): slot_precond[back_pick]]
    select_n x6 -> x0, other arithmetic: 8.8 us -> none  [the longest x1 7.49 us: body(): jnp.where(back_present[:, None, None], slot_precond[back_pick], 0.0)]
  transfers between devices with their start and end apart: 5 -> 0, of which waited for: 5 -> 0; matrix products, arithmetic and copies ran while one was open for 5% -> 0% of each run, Pallas kernels for 0% -> 0%
where the time goes in v1:
time: 135 us
  Pallas kernels  124 us (92%)
  other arithmetic  6.03 us (4%)
  local copies, waits for them, and re-layouts  3.43 us (3%)
    pallas_call x1, Pallas kernels, body(): pl.pallas_call(kernel, out_shape=(jax.ShapeDtypeStruct((2, band, width),...  124 us
    add x1, other arithmetic, body(): BETA_STAT * right_stats + (1.0 - BETA_STAT) * gram_right.astype(f32)  5.4 us
    unnamed x11, local copies, waits for them, and re-layouts  3.34 us

profile of v1, /device:TPU:1, one launch (start us, length us, event | category | flops | bytes accessed | tf_op | source)
XLA Modules:
  0.0 134.6 jit_solution(5152307746723609256)
XLA Ops:
  0.6 0.8 copy.13
  1.4 0.1 reshape.12.ob_ref
  1.5 0.0 copy-start.3
  1.5 0.6 select_reduce_fusion.inv_ref
  2.1 0.0 copy-done.3
  2.1 0.0 copy-start
  2.1 124.4 %shampoo.1 = (f32[2,128,1024]{2,1,0:T(8,128)}, f32[2,128,1024]{2,1,0:T(8,128)}, bf16[4,128,1024]{2,1,0:T(8,128)(2,1)}, bf16[4,128,1024]{2,1,0:T(8,128)(2,1)}) custom-call(s32[64]{0:T(128)} %copy-done.3, s32[32]{0:T(128)} %select_reduce_fusion.inv_ref, bf16[1,2,1024,1024]{3,2,1,0:T(8,128)(2,1)} %grads.1, f32[2,128,1024]{2,1,0:T(8,128)} %sm_hbm.1, ...), custom_call_target="tpu_custom_call" | custom-call | tf_op jit(solution)/shard_map/shampoo/pallas_call | solution.py:503
  126.6 0.0 copy-done
  126.6 0.0 copy-start.2
  126.6 5.4 %multiply_add_fusion = (f32[4,128,1024]{2,1,0:T(8,128)}, f32[4,128,1024]{2,1,0:T(8,128)}) fusion(bf16[4,128,1024]{2,1,0:T(8,128)(2,1)} %get-tuple-element.11, f32[4,128,1024]{2,1,0:T(8,128)S(1)} %copy-done, bf16[4,128,1024]{2,1,0:T(8,128)(2,1)} %get-tuple-element.10, f32[4,128,1024]{2,1,0:T(8,128)} %param.9), kind=kLoop, calls=%fused_computation | loop fusion | flops 4194304 | bytes 10485760 | tf_op jit(solution)/shard_map/add | solution.py:520
  132.0 0.0 copy-start.1
  132.0 0.0 copy-done.2
  132.0 1.0 copy.16
  133.0 0.6 copy-done.1
  133.6 1.0 copy.17
Async XLA Ops:
  1.5 0.6 copy-start.3
  2.1 124.5 %copy-start = (f32[4,128,1024]{2,1,0:T(8,128)S(1)}, f32[4,128,1024]{2,1,0:T(8,128)}, u32[]{:S(2)}) copy-start(f32[4,128,1024]{2,1,0:T(8,128)} %param.10) | copy-start | bytes 6291460
  126.6 5.4 %copy-start.2 = (f32[2,128,1024]{2,1,0:T(8,128)S(1)}, f32[2,128,1024]{2,1,0:T(8,128)}, u32[]{:S(2)}) copy-start(f32[2,128,1024]{2,1,0:T(8,128)} %get-tuple-element.18) | copy-start | bytes 3145732
  132.0 1.6 %copy-start.1 = (f32[2,128,1024]{2,1,0:T(8,128)S(1)}, f32[2,128,1024]{2,1,0:T(8,128)}, u32[]{:S(2)}) copy-start(f32[2,128,1024]{2,1,0:T(8,128)} %get-tuple-element.19) | copy-start | bytes 3145732

commit v2 on v1

--- a/solution.py
+++ b/solution.py
@@ -16,6 +16,9 @@
 NS = 4
 NK = 2
 Q = 4
+TILES = (0, 1, -2, 3, 4)
+SWAPPED = (1, 2, 3)
+TILE = 128
 
 
 def flip(v, low, high):
@@ -37,9 +40,9 @@
     smv, mom, gf, rf, tb, pv, lh, nsend, nrecv,
     r_own, r_v0, r_sa, r_ra, r_sb, r_rb, r_sc, r_rc,
     l_own, l_v0, l_sa, l_ra, l_sb, l_rb, l_sc, l_rc,
-    gl_h, gl_s, gl_r, gl_o, gr_h, gr_s, gr_r, gr_o,
+    gl_h, gl_s, gl_r, gl_o, gl_xs, gl_xr, gr_h, gr_s, gr_r, gr_o, gr_xs, gr_xr,
     loc_sem, a_ss, a_rs, gag_ss, gag_rs, rag_ss, rag_rs,
-    rp_ss, rp_rs, lp_ss, lp_rs, glp_ss, glp_rs, grp_ss, grp_rs, n_ss, n_rs,
+    rp_ss, rp_rs, lp_ss, lp_rs, glp_ss, glp_rs, grp_ss, grp_rs, xl_ss, xl_rs, xr_ss, xr_rs, n_ss, n_rs,
 ):
     band = sm_hbm.shape[1]
     width = sm_hbm.shape[2]
@@ -175,10 +178,11 @@
     right.start()
     left.start()
 
-    for j in (0, 1):
-        go(remote(grads.at[0, 1, rows(zm, j)], nr1.at[c], a_ss.at[4, j], a_rs.at[4, c], dev(zm, j)))
-        go(remote(grads.at[0, 0, rows(zp, j)], nr0.at[c], a_ss.at[5, j], a_rs.at[5, c], dev(zp, j)))
-
+    def near_send(j, there):
+        go(remote(grads.at[0, 1, rows(zm, there)], nr1.at[c], a_ss.at[4, j], a_rs.at[4, c], dev(zm, there)))
+        go(remote(grads.at[0, 0, rows(zp, there)], nr0.at[c], a_ss.at[5, j], a_rs.at[5, c], dev(zp, there)))
+
+    near_send(0, c)
     locs[4].wait()
     right.wait(0)
     right.send(1)
@@ -186,6 +190,7 @@
     for cc in (0, 1):
         arrived(far0.at[cc], a_ss.at[0, cc], a_rs.at[0, cc], dev(zm, cc))
         arrived(far1.at[cc], a_ss.at[1, cc], a_rs.at[1, cc], dev(zp, cc))
+    near_send(1, sib)
     arrived(sm0, a_ss.at[2, 0], a_rs.at[2, 0], dev(z, sib))
     arrived(sm1, a_ss.at[2, 1], a_rs.at[2, 1], dev(z, sib))
     locs[0].wait()
@@ -195,14 +200,18 @@
     def f32(v):
         return v.astype(jnp.float32)
 
-    @pl.loop(0, band // step_rows)
-    def _(i):
-        at = pl.ds(pl.multiple_of(i * step_rows, step_rows), step_rows)
-        ms0[at] = (f32(own0[at]) + f32(sm0[at])) + (f32(far0[0, at]) + f32(far0[1, at]))
-        ms1[at] = (f32(own1[at]) + f32(sm1[at])) + (f32(far1[0, at]) + f32(far1[1, at]))
-
-    go(remote(ms0, mg0, a_ss.at[6, 0], a_rs.at[6, 0], dev(zm, c)))
-    go(remote(ms1, mg1, a_ss.at[6, 1], a_rs.at[6, 1], dev(zp, c)))
+    half = band // 2
+    halves = [pl.ds(0, half), pl.ds(half, half)]
+    for h in (0, 1):
+        @pl.loop(0, half // step_rows)
+        def _(i, h=h):
+            at = pl.ds(pl.multiple_of(h * half + i * step_rows, step_rows), step_rows)
+            ms0[at] = (f32(own0[at]) + f32(sm0[at])) + (f32(far0[0, at]) + f32(far0[1, at]))
+            ms1[at] = (f32(own1[at]) + f32(sm1[at])) + (f32(far1[0, at]) + f32(far1[1, at]))
+
+        at = halves[h]
+        go(remote(ms0.at[at], mg0.at[at], a_ss.at[6 + h, 0], a_rs.at[6 + h, 0], dev(zm, c)))
+        go(remote(ms1.at[at], mg1.at[at], a_ss.at[6 + h, 1], a_rs.at[6 + h, 1], dev(zp, c)))
 
     locs[5].wait()
     left.wait(0)
@@ -216,9 +225,6 @@
     arrived(so, a_ss.at[3, 0], a_rs.at[3, 0], dev(z, sib))
     locs[2].wait()
     locs[3].wait()
-    arrived(mg0, a_ss.at[6, 0], a_rs.at[6, 0], dev(zm, c))
-    arrived(mg1, a_ss.at[6, 1], a_rs.at[6, 1], dev(zp, c))
-
     def fold(v):
         v = v[:8] + v[8:]
         total = v[:, :128]
@@ -226,65 +232,75 @@
             total = total + v[:, 128 * i:128 * (i + 1)]
         return total
 
-    for k, near, merged in ((0, nr0, mg0), (1, nr1, mg1)):
-        def one(i, acc, k=k, near=near, merged=merged):
-            start = pl.multiple_of(i * step_rows, step_rows)
-            at = pl.ds(start, step_rows)
-            g = (f32(ownb[k, at]) + f32(so[k, at])) + (f32(near[0, at]) + f32(near[1, at])) + merged[at]
-            m = BETA_MOMENT * smv[k, at] + (1.0 - BETA_MOMENT) * g * g
-            mom[k, at] = m
-            a = g / (jnp.sqrt(m) + EPS_ADAM)
-            gf[k, pl.ds(pl.multiple_of(r * band + start, step_rows), step_rows)] = g.astype(jnp.bfloat16)
-            return acc + fold(a * a)
-
-        nsend[k] = lax.fori_loop(0, band // step_rows, one, jnp.zeros((8, 128), jnp.float32))
+    def gradient(h):
+        at = halves[h]
+        arrived(mg0.at[at], a_ss.at[6 + h, 0], a_rs.at[6 + h, 0], dev(zm, c))
+        arrived(mg1.at[at], a_ss.at[6 + h, 1], a_rs.at[6 + h, 1], dev(zp, c))
+        for k, near, merged in ((0, nr0, mg0), (1, nr1, mg1)):
+            def one(i, acc, k=k, near=near, merged=merged):
+                start = pl.multiple_of(h * half + i * step_rows, step_rows)
+                at = pl.ds(start, step_rows)
+                g = (f32(ownb[k, at]) + f32(so[k, at])) + (f32(near[0, at]) + f32(near[1, at])) + merged[at]
+                m = BETA_MOMENT * smv[k, at] + (1.0 - BETA_MOMENT) * g * g
+                mom[k, at] = m
+                a = g / (jnp.sqrt(m) + EPS_ADAM)
+                gf[k, pl.ds(pl.multiple_of(r * band + start, step_rows), step_rows)] = g.astype(jnp.bfloat16)
+                return acc + fold(a * a)
+
+            before = jnp.zeros((8, 128), jnp.float32) if h == 0 else nsend[k]
+            nsend[k] = lax.fori_loop(0, half // step_rows, one, before)
 
     class Gather:
         def __init__(self, buf, ss, rs):
             self.buf, self.ss, self.rs = buf, ss, rs
 
-        def copy(self, i, k, zz, cc, to):
-            piece = self.buf.at[k, rows(zz, cc)]
-            return remote(piece, piece, self.ss.at[i], self.rs.at[i], to)
-
-        def got(self, i, k, zz, cc, to):
-            self.copy(i, k, zz, cc, to).wait_recv()
-
-        def start(self):
-            go(self.copy(0, 0, z, c, dev(zm, c)))
-            go(self.copy(1, 1, z, c, dev(zp, c)))
-            go(self.copy(2, 1, z, c, dev(zm, c)))
-            go(self.copy(3, 0, z, c, dev(zp, c)))
-            go(self.copy(4, 0, z, c, dev(z, sib)))
-            go(self.copy(5, 1, z, c, dev(z, sib)))
-
-        def forward(self):
-            self.got(0, 0, zp, c, dev(zm, c))
-            go(self.copy(6, 0, zp, c, dev(zm, c)))
-            self.got(1, 1, zm, c, dev(zp, c))
-            go(self.copy(7, 1, zm, c, dev(zp, c)))
-            go(self.copy(8, 0, zp, c, dev(z, sib)))
-            go(self.copy(9, 1, zm, c, dev(z, sib)))
-
-        def rest(self):
-            self.got(2, 1, zp, c, dev(zm, c))
-            go(self.copy(10, 1, zp, c, dev(z, sib)))
-            self.got(3, 0, zm, c, dev(zp, c))
-            go(self.copy(11, 0, zm, c, dev(z, sib)))
-
-        def last(self):
-            self.got(6, 0, zf, c, dev(zm, c))
-            go(self.copy(12, 0, zf, c, dev(z, sib)))
-            self.got(7, 1, zf, c, dev(zp, c))
-            go(self.copy(13, 1, zf, c, dev(z, sib)))
+        def copy(self, i, h, k, zz, cc, to):
+            at = pl.ds(pl.multiple_of((zz * 2 + cc) * band + h * half, half), half)
+            piece = self.buf.at[k, at]
+            return remote(piece, piece, self.ss.at[i, h], self.rs.at[i, h], to)
+
+        def got(self, i, h, k, zz, cc, to):
+            self.copy(i, h, k, zz, cc, to).wait_recv()
+
+        def start(self, h):
+            go(self.copy(0, h, 0, z, c, dev(zm, c)))
+            go(self.copy(1, h, 1, z, c, dev(zp, c)))
+            go(self.copy(2, h, 1, z, c, dev(zm, c)))
+            go(self.copy(3, h, 0, z, c, dev(zp, c)))
+            go(self.copy(4, h, 0, z, c, dev(z, sib)))
+            go(self.copy(5, h, 1, z, c, dev(z, sib)))
+
+        def forward(self, h):
+            self.got(0, h, 0, zp, c, dev(zm, c))
+            go(self.copy(6, h, 0, zp, c, dev(zm, c)))
+            self.got(1, h, 1, zm, c, dev(zp, c))
+            go(self.copy(7, h, 1, zm, c, dev(zp, c)))
+            go(self.copy(8, h, 0, zp, c, dev(z, sib)))
+            go(self.copy(9, h, 1, zm, c, dev(z, sib)))
+
+        def rest(self, h):
+            self.got(2, h, 1, zp, c, dev(zm, c))
+            go(self.copy(10, h, 1, zp, c, dev(z, sib)))
+            self.got(3, h, 0, zm, c, dev(zp, c))
+            go(self.copy(11, h, 0, zm, c, dev(z, sib)))
+
+        def last(self, h):
+            self.got(6, h, 0, zf, c, dev(zm, c))
+            go(self.copy(12, h, 0, zf, c, dev(z, sib)))
+            self.got(7, h, 1, zf, c, dev(zp, c))
+            go(self.copy(13, h, 1, zf, c, dev(z, sib)))
 
         def complete(self):
-            for i, k, zz in ((4, 0, z), (5, 1, z), (8, 0, zp), (9, 1, zm), (10, 1, zp), (11, 0, zm), (12, 0, zf), (13, 1, zf)):
-                self.got(i, k, zz, sib, dev(z, sib))
+            for h in (0, 1):
+                for i, k, zz in ((4, 0, z), (5, 1, z), (8, 0, zp), (9, 1, zm), (10, 1, zp), (11, 0, zm), (12, 0, zf), (13, 1, zf)):
+                    self.got(i, h, k, zz, sib, dev(z, sib))
 
     gather_g = Gather(gf, gag_ss, gag_rs)
     gather_r = Gather(rf, rag_ss, rag_rs)
-    gather_g.start()
+    gradient(0)
+    gather_g.start(0)
+    gradient(1)
+    gather_g.start(1)
     mom_cp = pltpu.make_async_copy(mom, moment_out, loc_sem.at[6])
     mom_cp.start()
 
@@ -292,23 +308,31 @@
     left.send(2)
     right.wait(2)
     right.send(3)
-    gather_g.forward()
+    gather_g.forward(0)
+    gather_g.forward(1)
     left.wait(2)
     left.send(3)
-    gather_g.rest()
+    gather_g.rest(0)
+    gather_g.rest(1)
     right.wait(3)
 
     def put_right(j, k, value):
         rf[k, pl.ds(pl.multiple_of(r * band + part * j, part), part)] = value
 
     right.finish(put_right)
-    gather_g.last()
-    gather_r.start()
+    gather_g.last(0)
+    gather_g.last(1)
+    gather_r.start(0)
+    gather_r.start(1)
     gather_g.complete()
 
+    def column(t):
+        return pl.ds(pl.multiple_of(((r + 8 + t) % 8) * TILE, TILE), TILE)
+
     class Outward:
-        def __init__(self, held, src, dst, out, ss, rs):
+        def __init__(self, held, src, dst, out, xs, xr, ss, rs, x_ss, x_rs):
             self.held, self.src, self.dst, self.out, self.ss, self.rs = held, src, dst, out, ss, rs
+            self.xs, self.xr, self.x_ss, self.x_rs = xs, xr, x_ss, x_rs
 
         def order(self, j):
             return [(j + i) % 4 for i in range(4)]
@@ -349,34 +373,41 @@
                     block, far, here = self.look(j, s, q)
                     value = jnp.where(far == 1, self.dst[j, q], here)
                     value = jnp.where(block < 32, value, jnp.zeros_like(value))
-                    self.out[q, pl.ds(part * j, part)] = value
-
-    out_l = Outward(gl_h, gl_s, gl_r, gl_o, glp_ss, glp_rs)
-    out_r = Outward(gr_h, gr_s, gr_r, gr_o, grp_ss, grp_rs)
+                    at = pl.ds(part * j, part)
+                    for i, t in enumerate(TILES):
+                        piece = value[:, TILE * i:TILE * (i + 1)]
+                        self.out[q, at, column(t)] = piece
+                        if i in SWAPPED:
+                            self.xs[SWAPPED.index(i), q, at] = piece
+            for i, t in enumerate(SWAPPED):
+                go(remote(self.xs.at[i], self.xr.at[i], self.x_ss.at[i], self.x_rs.at[i], ((r + 8 + TILES[t]) % 8, s)))
+
+        def swap(self):
+            for i, t in enumerate(SWAPPED):
+                arrived(self.xr.at[i], self.x_ss.at[i], self.x_rs.at[i], ((r + 8 + TILES[t]) % 8, s))
+                for q in range(NS):
+                    self.out[q, :, column(-TILES[t])] = self.xr[i, q].T
+
+    out_l = Outward(gl_h, gl_s, gl_r, gl_o, gl_xs, gl_xr, glp_ss, glp_rs, xl_ss, xl_rs)
+    out_r = Outward(gr_h, gr_s, gr_r, gr_o, gr_xs, gr_xr, grp_ss, grp_rs, xr_ss, xr_rs)
 
     tile = 256
     mm = functools.partial(lax.dot_general, preferred_element_type=jnp.float32)
+
+    def put_gram(held, k, i, g):
+        g = g.astype(jnp.bfloat16)
+        for j in range(Q):
+            held[j, k, :, pl.ds(TILE * i, TILE)] = g[part * j:part * (j + 1)]
+
     for k in range(NK):
-        band_rows = gf[k, pl.ds(pl.multiple_of(r * band, band), band)]
-
-        @pl.loop(0, width // tile)
-        def _(i, k=k, band_rows=band_rows):
-            at = pl.ds(pl.multiple_of(i * tile, tile), tile)
-            g = mm(band_rows, gf[k, at], (((1,), (1,)), ((), ()))).astype(jnp.bfloat16)
-            for j in range(Q):
-                gl_h[j, k, :, at] = g[part * j:part * (j + 1)]
-
+        band_rows = gf[k, column(0)]
+        for i, t in enumerate(TILES):
+            put_gram(gl_h, k, i, mm(band_rows, gf[k, column(t)], (((1,), (1,)), ((), ()))))
     out_l.spread(0)
     for k in range(NK):
-        cols = gf[k, :, pl.ds(pl.multiple_of(r * band, band), band)].T
-
-        @pl.loop(0, width // tile)
-        def _(i, k=k, cols=cols):
-            at = pl.ds(pl.multiple_of(i * tile, tile), tile)
-            g = mm(cols, gf[k, :, at], (((1,), (0,)), ((), ()))).astype(jnp.bfloat16)
-            for j in range(Q):
-                gr_h[j, k, :, at] = g[part * j:part * (j + 1)]
-
+        band_columns = gf[k, :, column(0)].T
+        for i, t in enumerate(TILES):
+            put_gram(gr_h, k, i, mm(band_columns, gf[k, :, column(t)], (((1,), (0,)), ((), ()))))
     out_r.spread(0)
 
     left.wait(3)
@@ -390,11 +421,13 @@
     out_l.spread(1)
     out_r.wait(0)
     out_r.spread(1)
-    gather_r.forward()
+    gather_r.forward(0)
+    gather_r.forward(1)
     out_l.wait(1)
     out_l.spread(2)
-    gather_r.rest()
-    gather_r.last()
+    for h in (0, 1):
+        gather_r.rest(h)
+        gather_r.last(h)
     out_r.wait(1)
     out_r.spread(2)
     gather_r.complete()
@@ -445,10 +478,12 @@
     out_r.send()
     out_l.wait(3)
     out_l.finish()
+    out_r.wait(3)
+    out_r.finish()
+    out_l.swap()
     gl_cp = pltpu.make_async_copy(gl_o, gl_out, loc_sem.at[8])
     gl_cp.start()
-    out_r.wait(3)
-    out_r.finish()
+    out_r.swap()
     gr_cp = pltpu.make_async_copy(gr_o, gr_out, loc_sem.at[9])
     gr_cp.start()
 
@@ -463,6 +498,7 @@
     band, width = second_moment.shape[1], second_moment.shape[2]
     full = 8 * band
     part = band // Q
+    sent = len(TILES) * TILE
     table = owner_blocks.reshape(-1)
     blocks = jnp.arange(32, dtype=jnp.int32)
     inverse = jnp.sum(
@@ -476,8 +512,9 @@
         V((Q, 2, part, width), bf16), V((Q, 2, part, width), bf16),
     ]
     outward = [
-        V((Q, 16, part, width), bf16), V((Q, NS, part, width), bf16),
-        V((Q, NS, part, width), bf16), V((NS, band, width), bf16),
+        V((Q, 16, part, sent), bf16), V((Q, NS, part, sent), bf16),
+        V((Q, NS, part, sent), bf16), V((NS, band, width), bf16),
+        V((len(SWAPPED), NS, TILE, TILE), bf16), V((len(SWAPPED), NS, TILE, TILE), bf16),
     ]
     scratch = (
         [V((2, band, width), bf16)] * 2
@@ -494,8 +531,9 @@
         + [V((2, band, width), bf16)]
         + [V((4, 8, 128), f32), V((8, 4, 8, 128), f32)]
         + inward + inward + outward + outward
-        + [D((10,)), D((7, 2)), D((7, 2)), D((14,)), D((14,)), D((14,)), D((14,))]
+        + [D((10,)), D((8, 2)), D((8, 2))] + [D((14, 2))] * 4
         + [D((4, Q))] * 8
+        + [D((len(SWAPPED),))] * 4
         + [D((7,)), D((8,))]
     )
     hbm = pl.BlockSpec(memory_space=pl.ANY)

time: 135 us -> 124 us (0.919)
  Pallas kernels: 124 us -> 113 us
    pallas_call x1, Pallas kernels: 124 us -> 113 us  [body(): pl.pallas_call(kernel, out_shape=(jax.ShapeDtypeStruct((2, band, width),...]
where the time goes in v2:
time: 124 us; the launch traced here: 123 us
  Pallas kernels  113 us (91%)
  other arithmetic  6.03 us (5%)
  local copies, waits for them, and re-layouts  3.43 us (3%)
    pallas_call x1, Pallas kernels, body(): pl.pallas_call(kernel, out_shape=(jax.ShapeDtypeStruct((2, band, width),...  113 us
    add x1, other arithmetic, body(): BETA_STAT * right_stats + (1.0 - BETA_STAT) * gram_right.astype(f32)  5.4 us
    unnamed x11, local copies, waits for them, and re-layouts  3.34 us

profile of v2, /device:TPU:1, one launch (start us, length us, event | category | flops | bytes accessed | tf_op | source)
XLA Modules:
  0.0 123.4 jit_solution(12593202972371542782)
XLA Ops:
  0.6 0.8 copy.13
  1.4 0.1 reshape.12.ob_ref
  1.5 0.0 copy-start.3
  1.5 0.6 select_reduce_fusion.inv_ref
  2.1 0.0 copy-done.3
  2.1 0.0 copy-start
  2.1 113.3 %shampoo.1 = (f32[2,128,1024]{2,1,0:T(8,128)}, f32[2,128,1024]{2,1,0:T(8,128)}, bf16[4,128,1024]{2,1,0:T(8,128)(2,1)}, bf16[4,128,1024]{2,1,0:T(8,128)(2,1)}) custom-call(s32[64]{0:T(128)} %copy-done.3, s32[32]{0:T(128)} %select_reduce_fusion.inv_ref, bf16[1,2,1024,1024]{3,2,1,0:T(8,128)(2,1)} %grads.1, f32[2,128,1024]{2,1,0:T(8,128)} %sm_hbm.1, ...), custom_call_target="tpu_custom_call" | custom-call | tf_op jit(solution)/shard_map/shampoo/pallas_call | solution.py:541
  115.4 0.0 copy-done
  115.4 0.0 copy-start.2
  115.4 5.4 %multiply_add_fusion = (f32[4,128,1024]{2,1,0:T(8,128)}, f32[4,128,1024]{2,1,0:T(8,128)}) fusion(bf16[4,128,1024]{2,1,0:T(8,128)(2,1)} %get-tuple-element.11, f32[4,128,1024]{2,1,0:T(8,128)S(1)} %copy-done, bf16[4,128,1024]{2,1,0:T(8,128)(2,1)} %get-tuple-element.10, f32[4,128,1024]{2,1,0:T(8,128)} %param.9), kind=kLoop, calls=%fused_computation | loop fusion | flops 4194304 | bytes 10485760 | tf_op jit(solution)/shard_map/add | solution.py:558
  120.8 0.0 copy-start.1
  120.8 0.0 copy-done.2
  120.8 1.0 copy.16
  121.8 0.6 copy-done.1
  122.4 1.0 copy.17
Async XLA Ops:
  1.5 0.6 copy-start.3
  2.1 113.3 %copy-start = (f32[4,128,1024]{2,1,0:T(8,128)S(1)}, f32[4,128,1024]{2,1,0:T(8,128)}, u32[]{:S(2)}) copy-start(f32[4,128,1024]{2,1,0:T(8,128)} %param.10) | copy-start | bytes 6291460
  115.4 5.4 %copy-start.2 = (f32[2,128,1024]{2,1,0:T(8,128)S(1)}, f32[2,128,1024]{2,1,0:T(8,128)}, u32[]{:S(2)}) copy-start(f32[2,128,1024]{2,1,0:T(8,128)} %get-tuple-element.18) | copy-start | bytes 3145732
  120.8 1.6 %copy-start.1 = (f32[2,128,1024]{2,1,0:T(8,128)S(1)}, f32[2,128,1024]{2,1,0:T(8,128)}, u32[]{:S(2)}) copy-start(f32[2,128,1024]{2,1,0:T(8,128)} %get-tuple-element.19) | copy-start | bytes 3145732

commit v3 on v2

v3 whole, which is shorter than its diff:
```python
import functools

import jax
import jax.numpy as jnp
from jax import lax
from jax.experimental import pallas as pl
from jax.experimental.pallas import tpu as pltpu
from jax.sharding import PartitionSpec as P

BETA_STAT = 0.99
BETA_MOMENT = 0.95
EPS_ADAM = 1e-08
EPS_NORM = 1e-06
MESH = pl.DeviceIdType.MESH

NS = 4
NK = 2
Q = 4
TILES = (0, 1, -2, 3, 4)
SWAPPED = (1, 2, 3)
TILE = 128


def flip(v, low, high):
    if low:
        v = v + 1 - 2 * (v % 2)
    if high:
        v = 3 - v
    return v


def gray_bits(v):
    return ((v + 1) // 2) % 2, v // 2


def kernel(
    ob_ref, inv_ref, grads, sm_hbm, lroot, rroot,
    update_out, moment_out, gl_out, gr_out,
    far0, far1, sm0, sm1, nr0, nr1, so, mg0, mg1, ms0, ms1, own0, own1, ownb,
    smv, mom, gf, rf, tb, pv, lh, nsend, nrecv,
    r_own, r_v0, r_sa, r_ra, r_sb, r_rb, r_sc, r_rc,
    l_own, l_v0, l_sa, l_ra, l_sb, l_rb, l_sc, l_rc,
    gl_h, gl_s, gl_r, gl_o, gl_xs, gl_xr, gr_h, gr_s, gr_r, gr_o, gr_xs, gr_xr,
    loc_sem, a_ss, a_rs, gag_ss, gag_rs, rag_ss, rag_rs,
    rp_ss, rp_rs, lp_ss, lp_rs, glp_ss, glp_rs, grp_ss, grp_rs, xl_ss, xl_rs, xr_ss, xr_rs, n_ss, n_rs,
):
    band = sm_hbm.shape[1]
    width = sm_hbm.shape[2]
    part = band // Q
    r = lax.axis_index("replica")
    s = lax.axis_index("shard")
    z, c = r // 2, r % 2
    x, y = s // 4, s % 4
    zp, zm, zf = (z + 1) % 4, (z + 3) % 4, (z + 2) % 4
    sib = 1 - c

    def dev(zz, cc):
        return (zz * 2 + cc, s)

    def rows(zz, cc):
        return pl.ds((zz * 2 + cc) * band, band)

    half = band // 2

    def half_rows(zz, cc, h):
        return pl.ds(pl.multiple_of((zz * 2 + cc) * band + h * half, half), half)

    def shard_at(flips):
        return 4 * flip(x, 2 in flips, 3 in flips) + flip(y, 0 in flips, 1 in flips)

    def across(dim):
        return (r, shard_at((dim,)))

    def bits(shard):
        ya, yb = gray_bits(shard % 4)
        xa, xb = gray_bits(shard // 4)
        return (ya, yb, xa, xb)

    mine = bits(s)

    def remote(src, dst, ss, rs, to):
        return pltpu.make_async_remote_copy(
            src_ref=src, dst_ref=dst, send_sem=ss, recv_sem=rs, device_id=to, device_id_type=MESH
        )

    me = (r, s)

    def arrived(dst, ss, rs, to):
        remote(dst, dst, ss, rs, to).wait_recv()

    sends = []

    def go(cp):
        cp.start()
        sends.append(cp)

    locs = [
        pltpu.make_async_copy(grads.at[0, :, half_rows(zm, c, 0)], own0, loc_sem.at[0]),
        pltpu.make_async_copy(grads.at[0, :, half_rows(zp, c, 1)], own1, loc_sem.at[1]),
        pltpu.make_async_copy(grads.at[0, :, rows(z, c)], ownb, loc_sem.at[2]),
        pltpu.make_async_copy(sm_hbm, smv, loc_sem.at[3]),
        pltpu.make_async_copy(rroot, r_own, loc_sem.at[4]),
        pltpu.make_async_copy(lroot, l_own, loc_sem.at[5]),
    ]
    for cp in locs:
        cp.start()

    barrier = pltpu.get_barrier_semaphore()
    partners = [dev(z, sib)] + [dev(zz, cc) for zz in (zm, zp, zf) for cc in (0, 1)]
    partners += [across(d) for d in range(4)]
    for p in partners:
        pl.semaphore_signal(barrier, inc=1, device_id=p, device_id_type=MESH)
    pl.semaphore_wait(barrier, len(partners))

    def far_send(k):
        for j in (0, 1):
            go(remote(grads.at[0, k, half_rows(zf, j, 0)], far0.at[k, c], a_ss.at[k, 0, j], a_rs.at[k, 0, c], dev(zm, j)))
            go(remote(grads.at[0, k, half_rows(zf, j, 1)], far1.at[k, c], a_ss.at[k, 1, j], a_rs.at[k, 1, c], dev(zp, j)))

    def side_send(k):
        go(remote(grads.at[0, k, half_rows(zm, sib, 0)], sm0.at[k], a_ss.at[k, 2, 0], a_rs.at[k, 2, 0], dev(z, sib)))
        go(remote(grads.at[0, k, half_rows(zp, sib, 1)], sm1.at[k], a_ss.at[k, 2, 1], a_rs.at[k, 2, 1], dev(z, sib)))
        go(remote(grads.at[0, k, rows(z, sib)], so.at[k], a_ss.at[k, 3, 0], a_rs.at[k, 3, 0], dev(z, sib)))

    def near_send(k, j):
        there = (c, sib)[j]
        go(remote(grads.at[0, k, half_rows(zm, there, 1)], nr1.at[k, c], a_ss.at[k, 4, j], a_rs.at[k, 4, c], dev(zm, there)))
        go(remote(grads.at[0, k, half_rows(zp, there, 0)], nr0.at[k, c], a_ss.at[k, 5, j], a_rs.at[k, 5, c], dev(zp, there)))

    step_rows = 16

    def f32(v):
        return v.astype(jnp.float32)

    def far_wait(k):
        for cc in (0, 1):
            arrived(far0.at[k, cc], a_ss.at[k, 0, cc], a_rs.at[k, 0, cc], dev(zm, cc))
            arrived(far1.at[k, cc], a_ss.at[k, 1, cc], a_rs.at[k, 1, cc], dev(zp, cc))
        arrived(sm0.at[k], a_ss.at[k, 2, 0], a_rs.at[k, 2, 0], dev(z, sib))
        arrived(sm1.at[k], a_ss.at[k, 2, 1], a_rs.at[k, 2, 1], dev(z, sib))

    def merge(k):
        @pl.loop(0, half // step_rows)
        def _(i):
            at = pl.ds(pl.multiple_of(i * step_rows, step_rows), step_rows)
            ms0[k, at] = (f32(own0[k, at]) + f32(sm0[k, at])) + (f32(far0[k, 0, at]) + f32(far0[k, 1, at]))
            ms1[k, at] = (f32(own1[k, at]) + f32(sm1[k, at])) + (f32(far1[k, 0, at]) + f32(far1[k, 1, at]))

        go(remote(ms0.at[k], mg0.at[k], a_ss.at[k, 6, 0], a_rs.at[k, 6, 0], dev(zm, c)))
        go(remote(ms1.at[k], mg1.at[k], a_ss.at[k, 6, 1], a_rs.at[k, 6, 1], dev(zp, c)))

    def fold(v):
        v = v[:8] + v[8:]
        total = v[:, :128]
        for i in range(1, width // 128):
            total = total + v[:, 128 * i:128 * (i + 1)]
        return total

    def gradient(k):
        for cc in (0, 1):
            arrived(nr1.at[k, cc], a_ss.at[k, 4, cc], a_rs.at[k, 4, cc], dev(zm, cc))
            arrived(nr0.at[k, cc], a_ss.at[k, 5, cc], a_rs.at[k, 5, cc], dev(zp, cc))
        arrived(so.at[k], a_ss.at[k, 3, 0], a_rs.at[k, 3, 0], dev(z, sib))
        arrived(mg0.at[k], a_ss.at[k, 6, 0], a_rs.at[k, 6, 0], dev(zm, c))
        arrived(mg1.at[k], a_ss.at[k, 6, 1], a_rs.at[k, 6, 1], dev(zp, c))
        acc = jnp.zeros((8, 128), jnp.float32)
        for h, near, merged in ((0, nr0, mg0), (1, nr1, mg1)):
            def one(i, acc, h=h, near=near, merged=merged):
                inner = pl.ds(pl.multiple_of(i * step_rows, step_rows), step_rows)
                start = pl.multiple_of(h * half + i * step_rows, step_rows)
                at = pl.ds(start, step_rows)
                g = (f32(ownb[k, at]) + f32(so[k, at])) + (f32(near[k, 0, inner]) + f32(near[k, 1, inner])) + merged[k, inner]
                m = BETA_MOMENT * smv[k, at] + (1.0 - BETA_MOMENT) * g * g
                mom[k, at] = m
                a = g / (jnp.sqrt(m) + EPS_ADAM)
                gf[k, pl.ds(pl.multiple_of(r * band + start, step_rows), step_rows)] = g.astype(jnp.bfloat16)
                return acc + fold(a * a)

            acc = lax.fori_loop(0, half // step_rows, one, acc)
        nsend[k] = acc

    class Inward:
        def __init__(self, root, own, v0, sa, ra, sb, rb, sc, rc, ss, rs):
            self.root, self.own, self.v0 = root, own, v0
            self.bufs = [(sa, ra), (sb, rb), (sc, rc)]
            self.ss, self.rs = ss, rs

        def order(self, j):
            return [(j + i) % 4 for i in range(4)]

        def start(self):
            for j in range(Q):
                d = self.order(j)
                go(remote(self.root.at[:, pl.ds(part * j, part)], self.v0.at[j],
                          self.ss.at[0, j], self.rs.at[0, j], across(d[3])))

        def wait(self, stage):
            for j in range(Q):
                d = self.order(j)
                dst = self.v0.at[j] if stage == 0 else self.bufs[stage - 1][1].at[j]
                arrived(dst, self.ss.at[stage, j], self.rs.at[stage, j], across(d[3 - stage]))

        def pick(self, j, level, home_flips, k, ea, eb):
            d = self.order(j)
            place = inv_ref[2 * shard_at(home_flips) + k]
            owner, slot = place // NS, place % NS
            theirs = bits(owner)
            value = jnp.where(theirs[d[3]] != mine[d[3]], self.v0[j, slot],
                              self.own[slot, pl.ds(part * j, part)])
            if level >= 1:
                value = jnp.where(theirs[d[2]] != mine[d[2]], self.bufs[0][1][j, ea], value)
            if level >= 2:
                value = jnp.where(theirs[d[1]] != mine[d[1]], self.bufs[1][1][j, eb], value)
            if level >= 3:
                value = jnp.where(theirs[d[0]] != mine[d[0]], self.bufs[2][1][j, k], value)
            return value

        def send(self, stage):
            src, dst = self.bufs[stage - 1]
            for j in range(Q):
                d = self.order(j)
                for e in range(8 >> (stage - 1)):
                    k, r0, r1 = e % 2, (e // 2) % 2, e // 4
                    if stage == 1:
                        flips = (d[2],) + ((d[0],) if r0 else ()) + ((d[1],) if r1 else ())
                        ea = eb = None
                    elif stage == 2:
                        flips = (d[1],) + ((d[0],) if r0 else ())
                        ea, eb = 4 + 2 * r0 + k, None
                    else:
                        flips = (d[0],)
                        ea, eb = 2 + k, 2 + k
                    src[j, e] = self.pick(j, stage - 1, flips, k, ea, eb)
                go(remote(src.at[j], dst.at[j], self.ss.at[stage, j], self.rs.at[stage, j], across(d[3 - stage])))

        def finish(self, put):
            for j in range(Q):
                for k in range(NK):
                    put(j, k, self.pick(j, 3, (), k, k, k))

    right = Inward(rroot, r_own, r_v0, r_sa, r_ra, r_sb, r_rb, r_sc, r_rc, rp_ss, rp_rs)
    left = Inward(lroot, l_own, l_v0, l_sa, l_ra, l_sb, l_rb, l_sc, l_rc, lp_ss, lp_rs)
    class Gather:
        def __init__(self, buf, ss, rs):
            self.buf, self.ss, self.rs = buf, ss, rs

        def copy(self, i, k, h, zz, cc, to):
            piece = self.buf.at[k, half_rows(zz, cc, h)]
            return remote(piece, piece, self.ss.at[i, k], self.rs.at[i, k], to)

        def got(self, i, k, h, zz, cc, to):
            self.copy(i, k, h, zz, cc, to).wait_recv()

        def start(self, k):
            go(self.copy(0, k, 0, z, c, dev(zm, c)))
            go(self.copy(1, k, 1, z, c, dev(zp, c)))
            go(self.copy(2, k, 1, z, c, dev(zm, c)))
            go(self.copy(3, k, 0, z, c, dev(zp, c)))
            go(self.copy(4, k, 0, z, c, dev(z, sib)))
            go(self.copy(5, k, 1, z, c, dev(z, sib)))

        def forward(self, k):
            self.got(0, k, 0, zp, c, dev(zm, c))
            go(self.copy(6, k, 0, zp, c, dev(zm, c)))
            self.got(1, k, 1, zm, c, dev(zp, c))
            go(self.copy(7, k, 1, zm, c, dev(zp, c)))
            go(self.copy(8, k, 0, zp, c, dev(z, sib)))
            go(self.copy(9, k, 1, zm, c, dev(z, sib)))

        def rest(self, k):
            self.got(2, k, 1, zp, c, dev(zm, c))
            go(self.copy(10, k, 1, zp, c, dev(z, sib)))
            self.got(3, k, 0, zm, c, dev(zp, c))
            go(self.copy(11, k, 0, zm, c, dev(z, sib)))

        def last(self, k):
            self.got(6, k, 0, zf, c, dev(zm, c))
            go(self.copy(12, k, 0, zf, c, dev(z, sib)))
            self.got(7, k, 1, zf, c, dev(zp, c))
            go(self.copy(13, k, 1, zf, c, dev(z, sib)))

        def complete(self, k):
            for i, h, zz in ((4, 0, z), (5, 1, z), (8, 0, zp), (9, 1, zm), (10, 1, zp), (11, 0, zm), (12, 0, zf), (13, 1, zf)):
                self.got(i, k, h, zz, sib, dev(z, sib))

    gather_g = Gather(gf, gag_ss, gag_rs)
    gather_r = Gather(rf, rag_ss, rag_rs)

    def put_right(j, k, value):
        rf[k, pl.ds(pl.multiple_of(r * band + part * j, part), part)] = value

    def put_left(j, k, value):
        lh[k, pl.ds(part * j, part)] = value

    def column(t):
        return pl.ds(pl.multiple_of(((r + 8 + t) % 8) * TILE, TILE), TILE)

    class Outward:
        def __init__(self, held, src, dst, out, xs, xr, ss, rs, x_ss, x_rs):
            self.held, self.src, self.dst, self.out, self.ss, self.rs = held, src, dst, out, ss, rs
            self.xs, self.xr, self.x_ss, self.x_rs = xs, xr, x_ss, x_rs

        def order(self, j):
            return [(j + i) % 4 for i in range(4)]

        def spread(self, k, stage):
            n = 1 << stage
            for j in range(Q):
                d = self.order(j)
                go(remote(self.held.at[j, k, pl.ds(0, n)], self.held.at[j, k, pl.ds(n, n)],
                          self.ss.at[3 * k + stage, j], self.rs.at[3 * k + stage, j], across(d[stage])))

        def wait(self, k, stage):
            n = 1 << stage
            for j in range(Q):
                d = self.order(j)
                arrived(self.held.at[j, k, pl.ds(n, n)], self.ss.at[3 * k + stage, j], self.rs.at[3 * k + stage, j], across(d[stage]))

        def wait_last(self):
            for j in range(Q):
                d = self.order(j)
                arrived(self.dst.at[j], self.ss.at[6, j], self.rs.at[6, j], across(d[3]))

        def look(self, j, owner, q):
            d = self.order(j)
            block = ob_ref[owner * NS + q]
            safe = jnp.minimum(block, 31)
            theirs = bits(safe // 2)
            differ = [jnp.where(theirs[t] != mine[t], 1, 0) for t in d]
            return block, differ[3], self.held[j, safe % 2, differ[0] + 2 * differ[1] + 4 * differ[2]]

        def send(self):
            for j in range(Q):
                d = self.order(j)
                for q in range(NS):
                    self.src[j, q] = self.look(j, shard_at((d[3],)), q)[2]
                go(remote(self.src.at[j], self.dst.at[j], self.ss.at[6, j], self.rs.at[6, j], across(d[3])))

        def finish(self):
            for j in range(Q):
                for q in range(NS):
                    block, far, here = self.look(j, s, q)
                    value = jnp.where(far == 1, self.dst[j, q], here)
                    value = jnp.where(block < 32, value, jnp.zeros_like(value))
                    at = pl.ds(part * j, part)
                    for i, t in enumerate(TILES):
                        piece = value[:, TILE * i:TILE * (i + 1)]
                        self.out[q, at, column(t)] = piece
                        if i in SWAPPED:
                            self.xs[SWAPPED.index(i), q, at] = piece
            for i, t in enumerate(SWAPPED):
                go(remote(self.xs.at[i], self.xr.at[i], self.x_ss.at[i], self.x_rs.at[i], ((r + 8 + TILES[t]) % 8, s)))

        def swap(self):
            for i, t in enumerate(SWAPPED):
                arrived(self.xr.at[i], self.x_ss.at[i], self.x_rs.at[i], ((r + 8 + TILES[t]) % 8, s))
                for q in range(NS):
                    self.out[q, :, column(-TILES[t])] = self.xr[i, q].T

    out_l = Outward(gl_h, gl_s, gl_r, gl_o, gl_xs, gl_xr, glp_ss, glp_rs, xl_ss, xl_rs)
    out_r = Outward(gr_h, gr_s, gr_r, gr_o, gr_xs, gr_xr, grp_ss, grp_rs, xr_ss, xr_rs)

    tile = 256
    mm = functools.partial(lax.dot_general, preferred_element_type=jnp.float32)

    def put_gram(held, k, i, g):
        g = g.astype(jnp.bfloat16)
        for j in range(Q):
            held[j, k, 0, :, pl.ds(TILE * i, TILE)] = g[part * j:part * (j + 1)]

    def gram_left(k):
        band_rows = gf[k, column(0)]
        for i, t in enumerate(TILES):
            put_gram(gl_h, k, i, mm(band_rows, gf[k, column(t)], (((1,), (1,)), ((), ()))))

    def gram_right(k):
        band_columns = gf[k, :, column(0)].T
        for i, t in enumerate(TILES):
            put_gram(gr_h, k, i, mm(band_columns, gf[k, :, column(t)], (((1,), (0,)), ((), ()))))

    def precondition(k):
        @pl.loop(0, width // tile)
        def _(i):
            at = pl.ds(pl.multiple_of(i * tile, tile), tile)
            tb[at] = mm(gf[k, at], rf[k], (((1,), (0,)), ((), ()))).astype(jnp.bfloat16)

        @pl.loop(0, width // tile)
        def _(i):
            at = pl.ds(pl.multiple_of(i * tile, tile), tile)
            pv[k, :, at] = mm(lh[k], tb[:, at], (((1,), (0,)), ((), ())))

        def square(i, acc):
            v = pv[k, pl.ds(pl.multiple_of(i * step_rows, step_rows), step_rows)]
            return acc + fold(v * v)

        nsend[NK + k] = lax.fori_loop(0, band // step_rows, square, jnp.zeros((8, 128), jnp.float32))

    others = [(z, sib, 0)] + [(zz, cc, 1 + 2 * i + cc) for i, zz in enumerate((zm, zp, zf)) for cc in (0, 1)]

    def norms_send():
        for zz, cc, i in others:
            go(remote(nsend, nrecv.at[r], n_ss.at[i], n_rs.at[r], dev(zz, cc)))

    def norms_apply():
        for zz, cc, i in others:
            src = zz * 2 + cc
            arrived(nrecv.at[src], n_ss.at[i], n_rs.at[src], dev(zz, cc))
        nrecv[r] = nsend[...]
        sums = nrecv[0]
        for i in range(1, 8):
            sums = sums + nrecv[i]
        for k in range(NK):
            adam_total = jnp.sum(sums[k], keepdims=True)
            pre_total = jnp.sum(sums[NK + k], keepdims=True)
            scaling = jnp.sqrt(adam_total) / (jnp.sqrt(pre_total) + EPS_NORM)

            @pl.loop(0, band // step_rows)
            def _(i, k=k, scaling=scaling):
                at = pl.ds(pl.multiple_of(i * step_rows, step_rows), step_rows)
                pv[k, at] = pv[k, at] * scaling

    mom_cp = pltpu.make_async_copy(mom, moment_out, loc_sem.at[6])
    up_cp = pltpu.make_async_copy(pv, update_out, loc_sem.at[7])
    gl_cp = pltpu.make_async_copy(gl_o, gl_out, loc_sem.at[8])
    gr_cp = pltpu.make_async_copy(gr_o, gr_out, loc_sem.at[9])

    far_send(0)
    side_send(0)
    near_send(0, 0)
    right.start()
    side_send(1)
    locs[0].wait()
    locs[1].wait()
    locs[4].wait()
    right.wait(0)
    right.send(1)
    left.start()
    far_wait(0)
    near_send(0, 1)
    merge(0)
    far_send(1)
    locs[5].wait()
    locs[2].wait()
    locs[3].wait()
    gradient(0)
    gather_g.start(0)
    near_send(1, 0)
    left.wait(0)
    left.send(1)
    right.wait(1)
    right.send(2)
    far_wait(1)
    merge(1)
    gather_g.forward(0)
    near_send(1, 1)
    gather_g.rest(0)
    gather_g.last(0)
    gather_g.complete(0)
    gram_left(0)
    out_l.spread(0, 0)
    gram_right(0)
    out_r.spread(0, 0)
    right.wait(2)
    right.send(3)
    out_l.wait(0, 0)
    out_l.spread(0, 1)
    out_r.wait(0, 0)
    out_r.spread(0, 1)
    gradient(1)
    gather_g.start(1)
    mom_cp.start()
    left.wait(1)
    left.send(2)
    right.wait(3)
    right.finish(put_right)
    gather_g.forward(1)
    gather_r.start(0)
    gather_g.rest(1)
    out_l.wait(0, 1)
    out_l.spread(0, 2)
    out_r.wait(0, 1)
    out_r.spread(0, 2)
    gather_g.last(1)
    gather_r.start(1)
    gather_g.complete(1)
    gram_left(1)
    out_l.spread(1, 0)
    gram_right(1)
    out_r.spread(1, 0)
    left.wait(2)
    left.send(3)
    gather_r.forward(0)
    out_l.wait(1, 0)
    out_l.spread(1, 1)
    out_r.wait(1, 0)
    out_r.spread(1, 1)
    gather_r.forward(1)
    gather_r.rest(0)
    gather_r.last(0)
    left.wait(3)
    left.finish(put_left)
    out_l.wait(1, 1)
    out_l.spread(1, 2)
    out_r.wait(1, 1)
    out_r.spread(1, 2)
    gather_r.rest(1)
    gather_r.last(1)
    gather_r.complete(0)
    precondition(0)
    out_l.wait(0, 2)
    out_r.wait(0, 2)
    out_l.wait(1, 2)
    out_l.send()
    out_r.wait(1, 2)
    out_r.send()
    gather_r.complete(1)
    precondition(1)
    norms_send()
    out_l.wait_last()
    out_l.finish()
    out_r.wait_last()
    out_r.finish()
    norms_apply()
    up_cp.start()
    out_l.swap()
    gl_cp.start()
    out_r.swap()
    gr_cp.start()

    for cp in sends:
        cp.wait_send()
    for cp in (mom_cp, up_cp, gl_cp, gr_cp):
        cp.wait()


def body(grads, second_moment, left_stats, right_stats, left_root, right_root, owner_blocks):
    bf16, f32 = jnp.bfloat16, jnp.float32
    band, width = second_moment.shape[1], second_moment.shape[2]
    full = 8 * band
    part = band // Q
    half = band // 2
    sent = len(TILES) * TILE
    table = owner_blocks.reshape(-1)
    blocks = jnp.arange(32, dtype=jnp.int32)
    inverse = jnp.sum(
        jnp.where(table[None, :] == blocks[:, None], jnp.arange(64, dtype=jnp.int32)[None, :], 0), axis=1
    )
    V, D = pltpu.VMEM, pltpu.SemaphoreType.DMA
    inward = [
        V((NS, band, width), bf16), V((Q, NS, part, width), bf16),
        V((Q, 8, part, width), bf16), V((Q, 8, part, width), bf16),
        V((Q, 4, part, width), bf16), V((Q, 4, part, width), bf16),
        V((Q, 2, part, width), bf16), V((Q, 2, part, width), bf16),
    ]
    outward = [
        V((Q, NK, 8, part, sent), bf16), V((Q, NS, part, sent), bf16),
        V((Q, NS, part, sent), bf16), V((NS, band, width), bf16),
        V((len(SWAPPED), NS, TILE, TILE), bf16), V((len(SWAPPED), NS, TILE, TILE), bf16),
    ]
    scratch = (
        [V((NK, 2, half, width), bf16)] * 2
        + [V((NK, half, width), bf16)] * 2
        + [V((NK, 2, half, width), bf16)] * 2
        + [V((NK, band, width), bf16)]
        + [V((NK, half, width), f32)] * 4
        + [V((NK, half, width), bf16)] * 2
        + [V((NK, band, width), bf16)]
        + [V((2, band, width), f32)] * 2
        + [V((2, full, width), bf16)] * 2
        + [V((full, width), bf16)]
        + [V((2, band, width), f32)]
        + [V((2, band, width), bf16)]
        + [V((4, 8, 128), f32), V((8, 4, 8, 128), f32)]
        + inward + inward + outward + outward
        + [D((10,)), D((NK, 7, 2)), D((NK, 7, 2))] + [D((14, 2))] * 4
        + [D((4, Q))] * 4
        + [D((7, Q))] * 4
        + [D((len(SWAPPED),))] * 4
        + [D((7,)), D((8,))]
    )
    hbm = pl.BlockSpec(memory_space=pl.ANY)
    smem = pl.BlockSpec(memory_space=pltpu.SMEM)
    update, moment_new, gram_left, gram_right = pl.pallas_call(
        kernel,
        out_shape=(
            jax.ShapeDtypeStruct((2, band, width), f32),
            jax.ShapeDtypeStruct((2, band, width), f32),
            jax.ShapeDtypeStruct((NS, band, width), bf16),
            jax.ShapeDtypeStruct((NS, band, width), bf16),
        ),
        in_specs=[smem, smem, hbm, hbm, hbm, hbm],
        out_specs=(hbm, hbm, hbm, hbm),
        scratch_shapes=scratch,
        compiler_params=pltpu.CompilerParams(
            collective_id=0, has_side_effects=True, vmem_limit_bytes=50 * 2**20
        ),
        name="shampoo",
    )(table, inverse, grads, second_moment, left_root, right_root)
    left_new = BETA_STAT * left_stats + (1.0 - BETA_STAT) * gram_left.astype(f32)
    right_new = BETA_STAT * right_stats + (1.0 - BETA_STAT) * gram_right.astype(f32)
    return (update, moment_new, left_new, right_new)


def solution(mesh):
    in_specs = (
        P("replica", "shard", None, None),
        P("shard", "replica", None),
        P("shard", "replica", None),
        P("shard", "replica", None),
        P("shard", "replica", None),
        P("shard", "replica", None),
        P(),
    )
    out_specs = (
        P("shard", "replica", None),
        P("shard", "replica", None),
        P("shard", "replica", None),
        P("shard", "replica", None),
    )
    return jax.shard_map(body, mesh=mesh, in_specs=in_specs, out_specs=out_specs, check_vma=False)
```

time: 124 us -> 120 us (0.968)
  other arithmetic: 6.03 us -> 4.15 us
    pallas_call x1, Pallas kernels: 113 us -> 112 us  [body(): pl.pallas_call(kernel, out_shape=(jax.ShapeDtypeStruct((2, band, width),...]
    add x1, other arithmetic: 5.4 us -> 4.04 us  [body(): BETA_STAT * right_stats + (1.0 - BETA_STAT) * gram_right.astype(f32)]
    unnamed x11 -> x7, local copies, waits for them, and re-layouts: 3.34 us -> 2.71 us
where the time goes in v3:
time: 120 us; the launch traced here: 119 us
  Pallas kernels  112 us (93%)
  other arithmetic  4.15 us (3%)
  local copies, waits for them, and re-layouts  2.8 us (2%)
    pallas_call x1, Pallas kernels, body(): pl.pallas_call(kernel, out_shape=(jax.ShapeDtypeStruct((2, band, width),...  112 us
    add x1, other arithmetic, body(): BETA_STAT * right_stats + (1.0 - BETA_STAT) * gram_right.astype(f32)  4.04 us
    unnamed x7, local copies, waits for them, and re-layouts  2.71 us

profile of v3, /device:TPU:1, one launch (start us, length us, event | category | flops | bytes accessed | tf_op | source)
XLA Modules:
  0.0 119.4 jit_solution(17774904855540203139)
XLA Ops:
  0.6 0.8 copy.13
  1.4 0.1 reshape.12.ob_ref
  1.5 0.1 select_reduce_fusion.inv_ref
  1.6 0.0 copy-start
  1.6 0.0 copy-start.1
  1.6 111.7 %shampoo.1 = (f32[2,128,1024]{2,1,0:T(8,128)S(1)}, f32[2,128,1024]{2,1,0:T(8,128)S(1)}, bf16[4,128,1024]{2,1,0:T(8,128)(2,1)S(1)}, bf16[4,128,1024]{2,1,0:T(8,128)(2,1)}) custom-call(s32[64]{0:T(128)S(1)} %reshape.12.ob_ref, s32[32]{0:T(128)S(1)} %select_reduce_fusion.inv_ref, bf16[1,2,1024,1024]{3,2,1,0:T(8,128)(2,1)} %grads.1, f32[2,128,1024]{2,1,0:T(8,128)} %sm_hbm.1, ...), custom_call_target="tpu_custom_call" | custom-call | tf_op jit(solution)/shard_map/shampoo/pallas_call | solution.py:583
  113.4 0.0 copy-done
  113.4 0.0 copy-done.1
  113.4 4.0 %multiply_add_fusion = (f32[4,128,1024]{2,1,0:T(8,128)}, f32[4,128,1024]{2,1,0:T(8,128)}) fusion(bf16[4,128,1024]{2,1,0:T(8,128)(2,1)} %get-tuple-element.11, f32[4,128,1024]{2,1,0:T(8,128)S(1)} %copy-done, bf16[4,128,1024]{2,1,0:T(8,128)(2,1)S(1)} %get-tuple-element.10, f32[4,128,1024]{2,1,0:T(8,128)S(1)} %copy-done.1), kind=kLoop, calls=%fused_computation | loop fusion | flops 4194304 | bytes 10485760 | tf_op jit(solution)/shard_map/add | solution.py:600
  117.4 1.0 copy.16
  118.4 1.0 copy.17
Async XLA Ops:
  1.6 111.8 %copy-start = (f32[4,128,1024]{2,1,0:T(8,128)S(1)}, f32[4,128,1024]{2,1,0:T(8,128)}, u32[]{:S(2)}) copy-start(f32[4,128,1024]{2,1,0:T(8,128)} %param.10) | copy-start | bytes 6291460
  1.6 111.8 %copy-start.1 = (f32[4,128,1024]{2,1,0:T(8,128)S(1)}, f32[4,128,1024]{2,1,0:T(8,128)}, u32[]{:S(2)}) copy-start(f32[4,128,1024]{2,1,0:T(8,128)} %param.9) | copy-start | bytes 6291460

commit v4 on v3

--- a/solution.py
+++ b/solution.py
@@ -455,6 +455,9 @@
     near_send(1, 1)
     gather_g.rest(0)
     gather_g.last(0)
+    gradient(1)
+    gather_g.start(1)
+    mom_cp.start()
     gather_g.complete(0)
     gram_left(0)
     out_l.spread(0, 0)
@@ -462,27 +465,24 @@
     out_r.spread(0, 0)
     right.wait(2)
     right.send(3)
+    gather_g.forward(1)
+    left.wait(1)
+    left.send(2)
+    gather_g.rest(1)
     out_l.wait(0, 0)
     out_l.spread(0, 1)
     out_r.wait(0, 0)
     out_r.spread(0, 1)
-    gradient(1)
-    gather_g.start(1)
-    mom_cp.start()
-    left.wait(1)
-    left.send(2)
+    gather_g.last(1)
     right.wait(3)
     right.finish(put_right)
-    gather_g.forward(1)
     gather_r.start(0)
-    gather_g.rest(1)
     out_l.wait(0, 1)
     out_l.spread(0, 2)
     out_r.wait(0, 1)
     out_r.spread(0, 2)
-    gather_g.last(1)
+    gather_g.complete(1)
     gather_r.start(1)
-    gather_g.complete(1)
     gram_left(1)
     out_l.spread(1, 0)
     gram_right(1)

time: 120 us -> 120 us (level)
  no operation moved by 1% of the time
where the time goes in v4:
time: 120 us; the launch traced here: 119 us
  Pallas kernels  112 us (93%)
  other arithmetic  4.15 us (3%)
  local copies, waits for them, and re-layouts  2.8 us (2%)
    pallas_call x1, Pallas kernels, body(): pl.pallas_call(kernel, out_shape=(jax.ShapeDtypeStruct((2, band, width),...  112 us
    add x1, other arithmetic, body(): BETA_STAT * right_stats + (1.0 - BETA_STAT) * gram_right.astype(f32)  4.04 us
    unnamed x7, local copies, waits for them, and re-layouts  2.71 us

profile of v4, /device:TPU:1, one launch (start us, length us, event | category | flops | bytes accessed | tf_op | source)
XLA Modules:
  0.0 119.4 jit_solution(6618643436137982151)
XLA Ops:
  0.6 0.8 copy.13
  1.4 0.1 reshape.12.ob_ref
  1.5 0.1 select_reduce_fusion.inv_ref
  1.6 0.0 copy-start
  1.6 0.0 copy-start.1
  1.6 111.8 %shampoo.1 = (f32[2,128,1024]{2,1,0:T(8,128)S(1)}, f32[2,128,1024]{2,1,0:T(8,128)S(1)}, bf16[4,128,1024]{2,1,0:T(8,128)(2,1)S(1)}, bf16[4,128,1024]{2,1,0:T(8,128)(2,1)}) custom-call(s32[64]{0:T(128)S(1)} %reshape.12.ob_ref, s32[32]{0:T(128)S(1)} %select_reduce_fusion.inv_ref, bf16[1,2,1024,1024]{3,2,1,0:T(8,128)(2,1)} %grads.1, f32[2,128,1024]{2,1,0:T(8,128)} %sm_hbm.1, ...), custom_call_target="tpu_custom_call" | custom-call | tf_op jit(solution)/shard_map/shampoo/pallas_call | solution.py:583
  113.4 0.0 copy-done
  113.5 0.0 copy-done.1
  113.5 4.0 %multiply_add_fusion = (f32[4,128,1024]{2,1,0:T(8,128)}, f32[4,128,1024]{2,1,0:T(8,128)}) fusion(bf16[4,128,1024]{2,1,0:T(8,128)(2,1)} %get-tuple-element.11, f32[4,128,1024]{2,1,0:T(8,128)S(1)} %copy-done, bf16[4,128,1024]{2,1,0:T(8,128)(2,1)S(1)} %get-tuple-element.10, f32[4,128,1024]{2,1,0:T(8,128)S(1)} %copy-done.1), kind=kLoop, calls=%fused_computation | loop fusion | flops 4194304 | bytes 10485760 | tf_op jit(solution)/shard_map/add | solution.py:600
  117.5 1.0 copy.16
  118.5 1.0 copy.17
Async XLA Ops:
  1.6 111.9 %copy-start = (f32[4,128,1024]{2,1,0:T(8,128)S(1)}, f32[4,128,1024]{2,1,0:T(8,128)}, u32[]{:S(2)}) copy-start(f32[4,128,1024]{2,1,0:T(8,128)} %param.10) | copy-start | bytes 6291460
  1.6 111.9 %copy-start.1 = (f32[4,128,1024]{2,1,0:T(8,128)S(1)}, f32[4,128,1024]{2,1,0:T(8,128)}, u32[]{:S(2)}) copy-start(f32[4,128,1024]{2,1,0:T(8,128)} %param.9) | copy-start | bytes 6291460

commit v5 on v4

--- a/solution.py
+++ b/solution.py
@@ -379,10 +379,11 @@
             put_gram(gr_h, k, i, mm(band_columns, gf[k, :, column(t)], (((1,), (0,)), ((), ()))))
 
     def precondition(k):
-        @pl.loop(0, width // tile)
+        @pl.loop(0, 4)
         def _(i):
-            at = pl.ds(pl.multiple_of(i * tile, tile), tile)
-            tb[at] = mm(gf[k, at], rf[k], (((1,), (0,)), ((), ()))).astype(jnp.bfloat16)
+            at = pl.ds(pl.multiple_of((i // 2) * 512, 512), 512)
+            columns = pl.ds(pl.multiple_of((i % 2) * 512, 512), 512)
+            tb[at, columns] = mm(gf[k, at], rf[k, :, columns], (((1,), (0,)), ((), ()))).astype(jnp.bfloat16)
 
         @pl.loop(0, width // tile)
         def _(i):

time: 120 us -> 120 us (level)
  no operation moved by 1% of the time
where the time goes in v5:
time: 120 us; the launch traced here: 119 us
  Pallas kernels  112 us (93%)
  other arithmetic  4.15 us (3%)
  local copies, waits for them, and re-layouts  2.8 us (2%)
    pallas_call x1, Pallas kernels, body(): pl.pallas_call(kernel, out_shape=(jax.ShapeDtypeStruct((2, band, width),...  112 us
    add x1, other arithmetic, body(): BETA_STAT * right_stats + (1.0 - BETA_STAT) * gram_right.astype(f32)  4.04 us
    unnamed x7, local copies, waits for them, and re-layouts  2.71 us

profile of v5, /device:TPU:1, one launch (start us, length us, event | category | flops | bytes accessed | tf_op | source)
XLA Modules:
  0.0 119.4 jit_solution(12649457801769251434)
XLA Ops:
  0.6 0.8 copy.13
  1.4 0.1 reshape.12.ob_ref
  1.5 0.1 select_reduce_fusion.inv_ref
  1.6 0.0 copy-start
  1.6 0.0 copy-start.1
  1.6 111.8 %shampoo.1 = (f32[2,128,1024]{2,1,0:T(8,128)S(1)}, f32[2,128,1024]{2,1,0:T(8,128)S(1)}, bf16[4,128,1024]{2,1,0:T(8,128)(2,1)S(1)}, bf16[4,128,1024]{2,1,0:T(8,128)(2,1)}) custom-call(s32[64]{0:T(128)S(1)} %reshape.12.ob_ref, s32[32]{0:T(128)S(1)} %select_reduce_fusion.inv_ref, bf16[1,2,1024,1024]{3,2,1,0:T(8,128)(2,1)} %grads.1, f32[2,128,1024]{2,1,0:T(8,128)} %sm_hbm.1, ...), custom_call_target="tpu_custom_call" | custom-call | tf_op jit(solution)/shard_map/shampoo/pallas_call | solution.py:584
  113.4 0.0 copy-done
  113.5 0.0 copy-done.1
  113.5 4.0 %multiply_add_fusion = (f32[4,128,1024]{2,1,0:T(8,128)}, f32[4,128,1024]{2,1,0:T(8,128)}) fusion(bf16[4,128,1024]{2,1,0:T(8,128)(2,1)} %get-tuple-element.11, f32[4,128,1024]{2,1,0:T(8,128)S(1)} %copy-done, bf16[4,128,1024]{2,1,0:T(8,128)(2,1)S(1)} %get-tuple-element.10, f32[4,128,1024]{2,1,0:T(8,128)S(1)} %copy-done.1), kind=kLoop, calls=%fused_computation | loop fusion | flops 4194304 | bytes 10485760 | tf_op jit(solution)/shard_map/add | solution.py:601
  117.5 1.0 copy.16
  118.5 1.0 copy.17
Async XLA Ops:
  1.6 111.9 %copy-start = (f32[4,128,1024]{2,1,0:T(8,128)S(1)}, f32[4,128,1024]{2,1,0:T(8,128)}, u32[]{:S(2)}) copy-start(f32[4,128,1024]{2,1,0:T(8,128)} %param.10) | copy-start | bytes 6291460
  1.6 111.9 %copy-start.1 = (f32[4,128,1024]{2,1,0:T(8,128)S(1)}, f32[4,128,1024]{2,1,0:T(8,128)}, u32[]{:S(2)}) copy-start(f32[4,128,1024]{2,1,0:T(8,128)} %param.9) | copy-start | bytes 6291460
